TPU v7x, 128 devices: a whole 4x4x4 slice. The times are simulated.
128 devices in a mesh: seq: 32 (over y, x, core), ch: 4 (over z).
Axes of the slice: x: 4, y: 4, z: 4, core: 2. Of those that a mesh axis runs over, the one named last changes fastest.
Arguments:
- tokens: bfloat16 [131072, 512], P('seq', 'ch'), may hold values from -6 to 6
- norm_gain: float32 [512], P('ch'), may hold values from 0.5 to 2
- low_taps: float32 [15, 2, 512], P(None, None, 'ch'), may hold values from 0.45 to 0.75
- high_taps: float32 [15, 2, 512], P(None, None, 'ch'), may hold values from -3 to 3
- level_gain: float32 [16, 512], P(None, 'ch'), may hold values from -3 to 3
- mixing: bfloat16 [512, 512], replicated, may hold values from -0.25 to 0.25
- lengths: int32 [16], replicated, may hold values from 1 to 32768, 131072 in all
- cotangent: bfloat16 [131072, 512], P('seq', 'ch'), may hold values from -6 to 6
Outputs:
- layer_out: bfloat16 [131072, 512], P('seq', 'ch')
- grad_in: bfloat16 [131072, 512], P('seq', 'ch')
- weight_grad: float32 [512, 512], P('ch', 'seq')
Inputs may be any that keep to these rules, and one draw needn't show every extreme that they name: `lengths`: the segments fill the 131072 bases exactly; the longest has exactly 32768 bases.
All inputs are finite; a program needn't handle non-finite values.
Results may differ from a plain program's by a relative error of at most 0.0035.
Values may be sent and summed in bfloat16 or wider, within the bound.
No kernel may reach another device: no remote copies, remote signals or barrier semaphores. Data moves between devices by JAX's collectives and lax.ppermute only.
A program may use at most 320 MiB of HBM per device.

v0:
```python
import functools
import math

import jax
import jax.numpy as jnp
from jax import lax
from jax.experimental import pallas as pl
from jax.experimental.pallas import tpu as pltpu
from jax.sharding import PartitionSpec as P

LEVELS = 15
LANES = 128
NCH = 4
SEQ = 32
ZN = 4
ROWS = 1024
LOCAL = 32
FWD = 4
BWD = 4
EPS = 1e-06
GAP = 8
SCALE = 2048.0
F32 = jnp.float32
BF16 = jnp.bfloat16
VMEM = pltpu.VMEM
SMEM = pltpu.SMEM


def params():
    return pltpu.CompilerParams(vmem_limit_bytes=16 * 1024 * 1024)


def vspec():
    return pl.BlockSpec(memory_space=VMEM)


def sspec():
    return pl.BlockSpec(memory_space=SMEM)


def cost():
    return pl.CostEstimate(flops=1000, bytes_accessed=1000, transcendentals=0)


def turn_kernel(x_ref, xt_ref, scr):
    for m in range(LOCAL):
        j = m % 4 * 8 + m // 4
        t = x_ref[m * LANES : (m + 1) * LANES, :].astype(F32).T
        scr[j * (LANES + GAP) : j * (LANES + GAP) + LANES, :] = t
    for g in range(SEQ):
        for i in range(NCH):
            xt_ref[g, i] = scr[pl.ds(i * SEQ + g, LOCAL, stride=LANES + GAP), :].astype(BF16)


def turn(x):
    return pl.pallas_call(
        turn_kernel,
        out_shape=jax.ShapeDtypeStruct((SEQ, NCH, LOCAL, LANES), BF16),
        in_specs=[vspec()],
        out_specs=vspec(),
        scratch_shapes=[VMEM((LOCAL * (LANES + GAP), LANES), F32)],
        compiler_params=params(),
        cost_estimate=cost(),
        name="turn",
    )(x)


def prepare_kernel(len_ref, low_ref, high_ref, level_ref, gain_ref, rel_ref, table_ref):
    starts = []
    at = jnp.int32(0)
    for n in range(15):
        at = at + len_ref[n]
        starts.append(at)
    shape = (4, 8, LANES)
    base = (
        lax.broadcasted_iota(jnp.int32, shape, 0) * LANES
        + lax.broadcasted_iota(jnp.int32, shape, 1) * 512
        + lax.broadcasted_iota(jnp.int32, shape, 2)
    )

    def one(s, _):
        t = base + s * (LOCAL * LANES)
        start = jnp.zeros(shape, jnp.int32)
        for n in range(15):
            start = jnp.where(t >= starts[n], starts[n], start)
        rel_ref[s] = t - start
        return 0

    lax.fori_loop(0, SEQ, one, 0)

    scale = jnp.ones((1, LANES), F32)
    carried = jnp.zeros((1, LANES), F32)
    for k in range(LEVELS):
        low0, low1 = low_ref[k, 0:1], low_ref[k, 1:2]
        gain = level_ref[k : k + 1]
        ratio = gain * high_ref[k, 1:2] / low1
        table_ref[k : k + 1] = low1 / low0
        table_ref[16 + k : 17 + k] = (gain * high_ref[k, 0:1] - ratio * low0 + carried) * scale
        scale = scale * low0
        carried = ratio
    table_ref[LEVELS : LEVELS + 1] = gain_ref[...]
    table_ref[31:32] = (level_ref[LEVELS : LEVELS + 1] + carried) * scale


def prepare(lengths, low, high, level_gain, gain):
    return pl.pallas_call(
        prepare_kernel,
        out_shape=(
            jax.ShapeDtypeStruct((SEQ, 4, 8, LANES), jnp.int32),
            jax.ShapeDtypeStruct((32, LANES), F32),
        ),
        in_specs=[sspec()] + [vspec()] * 4,
        out_specs=(vspec(), vspec()),
        compiler_params=params(),
        cost_estimate=cost(),
        name="prepare",
    )(lengths, low, high, level_gain, gain.reshape(1, LANES))


def grad_hidden_kernel(me_ref, mix_ref, *refs):
    cot_refs, (out_ref, scr) = refs[:ZN], refs[ZN:]
    for m in range(8):
        acc = None
        for k in range(ZN):
            c = (me_ref[0] + ZN - k) % ZN
            part = lax.dot_general(
                mix_ref[:, pl.ds(pl.multiple_of(c * LANES, LANES), LANES)],
                cot_refs[k][m * LANES : (m + 1) * LANES, :],
                (((1,), (1,)), ((), ())),
                preferred_element_type=F32,
            )
            acc = part if acc is None else acc + part
        scr[m * (512 + GAP) : m * (512 + GAP) + 512, :] = acc
    for g in range(SEQ):
        for c in range(ZN):
            rows = [scr[pl.ds(c * LANES + i * SEQ + g, 8, stride=512 + GAP), :] for i in range(NCH)]
            out_ref[g * ZN + c] = jnp.concatenate(rows, axis=0).astype(BF16)


def grad_hidden_of(me, mixing, cot_parts):
    return pl.pallas_call(
        grad_hidden_kernel,
        out_shape=jax.ShapeDtypeStruct((SEQ * ZN, 32, LANES), BF16),
        in_specs=[sspec()] + [vspec()] * (1 + ZN),
        out_specs=vspec(),
        scratch_shapes=[VMEM((8 * (512 + GAP), LANES), F32)],
        compiler_params=params(),
        cost_estimate=cost(),
        name="grad_hidden",
    )(me, mixing, *cot_parts)


def forward_kernel(FWD, x_ref, rel_ref, t_ref, hid_ref, slope_ref, near, far):
    near[...] = jnp.zeros_like(near)
    far[...] = jnp.zeros_like(far)
    lane = lax.broadcasted_iota(jnp.int32, (8, LANES), 1)
    sub = lax.broadcasted_iota(jnp.int32, (8, LANES), 0)

    def before(now, old, by):
        return jnp.concatenate([old, now], axis=0)[old.shape[0] - by :][: now.shape[0]]

    def step(b, _):
        s = b * FWD
        rel = rel_ref[pl.ds(s, FWD)]
        inside = [rel >= 2**k for k in range(LEVELS)]
        for pair in range(0, NCH, 2):
            hidden = []
            for i in (pair, pair + 1):
                z = x_ref[pl.ds(s, FWD), i] * (t_ref[LEVELS * NCH + i] / SCALE)
                z = z.reshape(FWD, 4, 8, LANES)
                y = t_ref[16 * NCH + i] * z
                for k in range(LEVELS):
                    d = 2**k
                    if k < 8:
                        last = z[:, 3]
                        prev = before(last, near[k, i, pl.ds(3, 1)], 1)
                        near[k, i, pl.ds(3, 1)] = last[FWD - 1 :]
                        first = pltpu.roll(jnp.where(sub == 7, prev, last), 1, 1)
                        back = jnp.concatenate([first[:, None], z[:, :3]], axis=1)
                        if d < LANES:
                            back = pltpu.roll(jnp.where(lane >= LANES - d, back, z), d, 3)
                    elif k == 8:
                        last = z[:, 2:]
                        prev = before(last, near[k, i, pl.ds(2, 2)][None], 1)
                        near[k, i, pl.ds(2, 2)] = last[FWD - 1]
                        first = pltpu.roll(jnp.where(sub == 7, prev, last), 1, 2)
                        back = jnp.concatenate([first, z[:, :2]], axis=1)
                    elif k < 12:
                        by = 2 ** (k - 9)
                        prev = before(z, near[k, i][None], 1)
                        near[k, i] = z[FWD - 1]
                        back = pltpu.roll(jnp.where(sub >= 8 - by, prev, z), by, 2)
                    else:
                        by = 2 ** (k - 12)
                        old = far[k - 12, i]
                        back = before(z, old, by)
                        far[k - 12, i] = jnp.concatenate([old, z], axis=0)[FWD:]
                    z = z + t_ref[k * NCH + i] * jnp.where(inside[k], back, 0.0)
                    y = y + t_ref[(k + 17) * NCH + i] * z
                cdf = 0.5 * (1.0 + lax.erf(y * 0.7071067811865476))
                density = jnp.exp(-0.5 * y * y) * 0.3989422804014327
                slope_ref[i, pl.ds(s, FWD)] = cdf + y * density
                hidden.append(y * cdf)
            hid_ref[pl.ds(s, FWD), :, pl.ds(pair * 8, 16), :] = jnp.concatenate(
                hidden, axis=2
            ).astype(BF16)
        return 0

    lax.fori_loop(0, SEQ // FWD, step, 0)


def forward(x, rel, table):
    return pl.pallas_call(
        functools.partial(forward_kernel, FWD),
        out_shape=(
            jax.ShapeDtypeStruct((SEQ, ZN, 32, LANES), BF16),
            jax.ShapeDtypeStruct((NCH, SEQ, 4, 8, LANES), F32),
        ),
        in_specs=[vspec(), vspec(), sspec()],
        out_specs=(vspec(), vspec()),
        scratch_shapes=[
            VMEM((12, NCH, 4, 8, LANES), F32),
            VMEM((3, NCH, 4, 4, 8, LANES), F32),
        ],
        compiler_params=params(),
        cost_estimate=cost(),
        name="forward",
    )(x, rel, table)


def backward_kernel(BWD, gh_ref, slope_ref, rel_ref, t_ref, out_ref, near, far):
    near[...] = jnp.zeros_like(near)
    far[...] = jnp.zeros_like(far)
    lane = lax.broadcasted_iota(jnp.int32, (8, LANES), 1)
    sub = lax.broadcasted_iota(jnp.int32, (8, LANES), 0)

    def after(now, old, by):
        return jnp.concatenate([now, old], axis=0)[by:][: now.shape[0]]

    def step(b, _):
        s = SEQ - BWD - b * BWD
        rel = rel_ref[pl.ds(s, BWD)]
        inside = [rel >= 2**k for k in range(LEVELS)]
        for pair in range(0, NCH, 2):
            block = gh_ref[pl.ds(s, BWD), :, pl.ds(pair * 8, 16), :].astype(F32)
            for i in (pair, pair + 1):
                grad = block[:, :, (i - pair) * 8 : (i - pair + 1) * 8]
                grad = grad * slope_ref[i, pl.ds(s, BWD)]
                v = t_ref[31 * NCH + i] * grad
                for k in range(LEVELS - 1, -1, -1):
                    d = 2**k
                    p = jnp.where(inside[k], v, 0.0)
                    if k < 8:
                        head = p[:, 0]
                        foll = after(head, near[k, i, pl.ds(0, 1)], 1)
                        near[k, i, pl.ds(0, 1)] = head[:1]
                        end = pltpu.roll(jnp.where(sub == 0, foll, head), 7, 1)
                        ahead = jnp.concatenate([p[:, 1:], end[:, None]], axis=1)
                        if d < LANES:
                            ahead = pltpu.roll(jnp.where(lane < d, ahead, p), LANES - d, 3)
                    elif k == 8:
                        head = p[:, :2]
                        foll = after(head, near[k, i, pl.ds(0, 2)][None], 1)
                        near[k, i, pl.ds(0, 2)] = head[0]
                        end = pltpu.roll(jnp.where(sub == 0, foll, head), 7, 2)
                        ahead = jnp.concatenate([p[:, 2:], end], axis=1)
                    elif k < 12:
                        by = 2 ** (k - 9)
                        foll = after(p, near[k, i][None], 1)
                        near[k, i] = p[0]
                        ahead = pltpu.roll(jnp.where(sub < by, foll, p), 8 - by, 2)
                    else:
                        by = 2 ** (k - 12)
                        old = far[k - 12, i]
                        ahead = after(p, old, by)
                        far[k - 12, i] = jnp.concatenate([p, old], axis=0)[:4]
                    v = v + t_ref[(k + 16) * NCH + i] * grad + t_ref[k * NCH + i] * ahead
                out_ref[pl.ds(s, BWD), i] = v.reshape(BWD, 32, LANES).astype(BF16)
        return 0

    lax.fori_loop(0, SEQ // BWD, step, 0)


def backward(gh, slope, rel, table):
    return pl.pallas_call(
        functools.partial(backward_kernel, BWD),
        out_shape=jax.ShapeDtypeStruct((SEQ, NCH, LOCAL, LANES), BF16),
        in_specs=[vspec(), vspec(), vspec(), sspec()],
        out_specs=vspec(),
        scratch_shapes=[
            VMEM((12, NCH, 4, 8, LANES), F32),
            VMEM((3, NCH, 4, 4, 8, LANES), F32),
        ],
        compiler_params=params(),
        cost_estimate=cost(),
        name="backward",
    )(gh, slope, rel, table)


def hidden_tiles(hid_ref, scr):
    def load(j, _):
        scr[pl.ds(pl.multiple_of(j * (128 + GAP), 8), 128), :] = (
            hid_ref[pl.ds(j * 4, 4)].astype(F32).reshape(128, LANES)
        )
        return 0

    lax.fori_loop(0, SEQ, load, 0, unroll=4)
    for m in range(8):
        rows = [
            scr[pl.ds(c * 32 + i * 8 + m, SEQ, stride=LANES + GAP), :]
            for c in range(ZN)
            for i in range(NCH)
        ]
        yield m, slice(m * LANES, (m + 1) * LANES), jnp.concatenate(rows, axis=0)


def weigh_kernel(me_ref, hid_ref, held_ref, *refs):
    wg_refs, (scr, acc) = refs[:ZN], refs[ZN:]
    for m, at, h in hidden_tiles(hid_ref, scr):
        hb = h.astype(BF16)
        for k in range(ZN):
            part = jnp.dot(hb, held_ref[k, at], preferred_element_type=F32)
            acc[k] = part if m == 0 else acc[k] + part
    for n in range(ZN):
        row = pl.multiple_of((me_ref[0] + n) % ZN * LANES, LANES)
        for k in range(ZN):
            column = pl.multiple_of((me_ref[0] + ZN - k) % ZN * LANES, LANES)
            t = acc[k, pl.ds(row, LANES), :].T
            wg_refs[n][pl.ds(column, LANES), :] = t.astype(wg_refs[n].dtype)


def weigh(me, hid, held):
    return pl.pallas_call(
        weigh_kernel,
        out_shape=tuple(jax.ShapeDtypeStruct((512, LANES), BF16 if n else F32) for n in range(ZN)),
        in_specs=[sspec(), vspec(), vspec()],
        out_specs=(vspec(),) * ZN,
        scratch_shapes=[
            VMEM((SEQ * (LANES + GAP), LANES), F32),
            VMEM((ZN, 512, LANES), F32),
        ],
        compiler_params=params(),
        cost_estimate=cost(),
        name="weigh",
    )(me, hid, held)


def mix_kernel(me_ref, hid_ref, mix_ref, *refs):
    out_refs, scr = refs[:ZN], refs[ZN]
    for m, at, h in hidden_tiles(hid_ref, scr):
        ht = h.T.astype(BF16)
        for n in range(ZN):
            column = pl.ds(pl.multiple_of((me_ref[0] + n) % ZN * LANES, LANES), LANES)
            part = jnp.dot(ht, mix_ref[:, column], preferred_element_type=F32)
            out_refs[n][at, :] = part.astype(BF16)


def mix(me, hid, mixing):
    return pl.pallas_call(
        mix_kernel,
        out_shape=tuple(jax.ShapeDtypeStruct((ROWS, LANES), BF16) for _ in range(ZN)),
        in_specs=[sspec(), vspec(), vspec()],
        out_specs=(vspec(),) * ZN,
        scratch_shapes=[VMEM((SEQ * (LANES + GAP), LANES), F32)],
        compiler_params=params(),
        cost_estimate=cost(),
        name="mix",
    )(me, hid, mixing)


def inner_kernel(v_ref, xt_ref, gain_ref, out_ref):
    def one(g, acc):
        for i in range(NCH):
            acc = acc + gain_ref[i * SEQ + g] * (v_ref[g, i].astype(F32) * xt_ref[g, i].astype(F32))
        return acc

    out_ref[...] = lax.fori_loop(0, SEQ, one, jnp.zeros((LOCAL, LANES), F32))


def inner(v, xt, gain):
    return pl.pallas_call(
        inner_kernel,
        out_shape=jax.ShapeDtypeStruct((LOCAL, LANES), F32),
        in_specs=[vspec(), vspec(), sspec()],
        out_specs=vspec(),
        compiler_params=params(),
        cost_estimate=cost(),
        name="inner",
    )(v, xt, gain)


def grad_in_kernel(v_ref, xt_ref, cot_ref, inv_ref, mean_ref, gain_ref, out_ref, scr):
    inv = inv_ref[...]
    scale = inv * inv * inv * mean_ref[...]

    for g in range(SEQ):
        for i in range(NCH):
            c = i * SEQ + g
            u = (gain_ref[c] * inv) * v_ref[g, i].astype(F32) - scale * xt_ref[g, i].astype(F32)
            scr[c * (LOCAL + GAP) : c * (LOCAL + GAP) + LOCAL, :] = u
    for m in range(LOCAL):
        at = slice(m * LANES, (m + 1) * LANES)
        u = scr[pl.ds(m % 4 * 8 + m // 4, LANES, stride=LOCAL + GAP), :].T
        out_ref[at, :] = (cot_ref[at, :].astype(F32) + u).astype(BF16)


def grad_in_of(v, xt, cot, inv, mean, gain):
    return pl.pallas_call(
        grad_in_kernel,
        out_shape=jax.ShapeDtypeStruct((LOCAL * LANES, LANES), BF16),
        in_specs=[vspec()] * 5 + [sspec()],
        out_specs=vspec(),
        scratch_shapes=[VMEM((LANES * (LOCAL + GAP), LANES), F32)],
        compiler_params=params(),
        cost_estimate=cost(),
        name="grad_in",
    )(v, xt, cot, inv, mean, gain)


def exchange(a, axes):
    return lax.all_to_all(a, axes, 0, 0, tiled=True)


def sum_over_ch(a):
    total = a
    for by in (1, 2, 3):
        total = total + turned(a, by)
    return total


def turned(a, by):
    return lax.ppermute(a, "ch", [(j, (j + by) % ZN) for j in range(ZN)]) if by else a


def parts_of(a, me):
    a = a.reshape(8, ZN, LANES, LANES)
    return [
        turned(
            lax.dynamic_index_in_dim(a, (me + k) % ZN, 1, False).reshape(ROWS, LANES), k
        )
        for k in range(ZN)
    ]


def whole_kernel(me_ref, x_ref, *refs):
    parts, out_ref = refs[:ZN], refs[ZN]
    for k in range(ZN):
        r = (me_ref[0] + ZN - k) % ZN
        for n in range(8):
            part = parts[k][n * LANES : (n + 1) * LANES, :].astype(F32)
            out_ref[n, r] = (x_ref[n, r].astype(F32) + part).astype(BF16)


def whole_of(x, parts, place):
    shape = (8, ZN, LANES, LANES)
    return pl.pallas_call(
        whole_kernel,
        out_shape=jax.ShapeDtypeStruct(shape, BF16),
        in_specs=[sspec()] + [vspec()] * (1 + ZN),
        out_specs=vspec(),
        compiler_params=params(),
        cost_estimate=cost(),
        name="whole",
    )(place, x.reshape(shape), *parts).reshape(LOCAL * LANES, LANES)


def after(later, first):
    return lax.optimization_barrier((later, first))[0]


def per_device(tokens, norm_gain, low_taps, high_taps, level_gain, mixing, lengths, cotangent):
    both = ("seq", "ch")
    g = lax.axis_index("seq")
    full = mixing.shape[0]
    bases = LOCAL * LANES * SEQ

    me = lax.axis_index("ch")
    place = me.reshape(1)

    x = tokens.astype(F32)
    squares = jnp.sum(x * x, axis=1).reshape(8, ZN, LANES).swapaxes(0, 1).reshape(LOCAL, LANES)
    inv = lax.rsqrt(sum_over_ch(squares) / full + EPS)
    cot_parts = parts_of(after(cotangent, squares), me)
    xt = turn(tokens)
    x_sent = (xt.astype(F32) * (inv * SCALE)).astype(jnp.float16)
    x_sent = exchange(x_sent, "seq")
    x_seq = x_sent.astype(F32)
    rel, table = prepare(lengths, low_taps, high_taps, level_gain, norm_gain)
    table = lax.dynamic_index_in_dim(table.reshape(32, NCH, SEQ), g, 2, False).reshape(-1)
    gh = grad_hidden_of(after(place, table), mixing, cot_parts)
    gh_seq = exchange(after(gh, x_sent), both).reshape(SEQ, ZN, 32, LANES)
    held = jnp.stack(cot_parts)
    hid, slope = forward(x_seq, rel, table)
    hid_rows = exchange(after(hid, gh_seq).reshape(SEQ * ZN, 32, LANES), both)
    v = exchange(after(backward(gh_seq, after(slope, held), rel, table), hid_rows), "seq")
    shares = weigh(place, hid_rows, held)
    own_first = shares[0]
    shares = [turned(shares[n], n).astype(F32) for n in range(ZN)]
    wg = shares[0] + shares[1] + shares[2] + shares[3]
    mixed = mix(after(place, own_first), hid_rows, mixing)
    parts = [turned(mixed[n], n) for n in range(ZN)]
    own = inner(v, xt, norm_gain)
    wg = exchange(after(wg, own).reshape(SEQ, 16, LANES), "seq")
    others = [turned(own, k) for k in range(1, ZN)]
    mean = (own + others[0] + others[1] + others[2]) / full
    grad_in = grad_in_of(v, xt, cotangent, inv, mean, norm_gain)
    weight_grad = jnp.sum(after(wg, grad_in), axis=0).T / math.sqrt(bases)
    layer_out = whole_of(tokens, parts, place)
    return (layer_out, grad_in, weight_grad)


def solution(mesh):
    in_specs = (
        P("seq", "ch"),
        P("ch"),
        P(None, None, "ch"),
        P(None, None, "ch"),
        P(None, "ch"),
        P(),
        P(),
        P("seq", "ch"),
    )
    out_specs = (P("seq", "ch"), P("seq", "ch"), P("ch", "seq"))
    return jax.shard_map(
        per_device, mesh=mesh, in_specs=in_specs, out_specs=out_specs, check_vma=False
    )
```

profile of v0, /device:TPU:2, one launch (start us, length us, event | category | flops | bytes accessed | tf_op | source)
XLA Modules:
  0.0 132.5 jit_solution(12644984153315096916)
XLA Ops:
  0.6 1.8 %multiply_reduce_fusion = f32[4096]{0:T(1024)S(1)} fusion(bf16[4096,128]{1,0:T(8,128)(2,1)} %x_ref.1), kind=kLoop, calls=%fused_computation.1 | loop fusion | flops 1568768 | bytes 1064960 | tf_op jit(solution)/shard_map/reduce_sum | solution.py:481
  2.5 4.1 %collective-permute-start.2 = (f32[32,128]{1,0:T(8,128)S(1)}, f32[32,128]{1,0:T(8,128)S(1)}, u32[]{:S(2)}, u32[]{:S(2)}) collective-permute-start(f32[32,128]{1,0:T(8,128)S(1)} %bitcast.50), channel_id=1, source_target_pairs={{0,3},{1,0},{2,1},{3,2},{4,7},{5,4},{6,5},{7,6},{8,11},{9,8},{10,9... | collective-permute-start | bytes 49160 | tf_op jit(solution)/shard_map/ppermute | solution.py:432
  6.6 1.3 collective-permute-start
  9.7 2.1 %collective-permute-done.1 = f32[32,128]{1,0:T(8,128)S(1)} collective-permute-done((f32[32,128]{1,0:T(8,128)S(1)}, f32[32,128]{1,0:T(8,128)S(1)}, u32[]{:S(2)}, u32[]{:S(2)}) %collective-permute-start.1) | collective-permute-done | bytes 16416 | tf_op jit(solution)/shard_map/ppermute | solution.py:432
  11.9 1.3 multiply_convert_fusion
  13.2 7.8 %all-to-all-start = ((f16[32,4,32,128]{3,2,1,0:T(8,128)(2,1)}), f16[32,4,32,128]{3,2,1,0:T(8,128)(2,1)}, u32[]{:S(2)}, u32[]{:S(2)}) async-start(f16[32,4,32,128]{3,2,1,0:T(8,128)(2,1)} %multiply_convert_fusion), calls=%async_computation | async-start | bytes 2097152 | tf_op jit(solution)/shard_map/all_to_all | solution.py:421
  22.0 2.0 %collective-permute-start.4 = (bf16[1024,128]{1,0:T(8,128)(2,1)}, bf16[1024,128]{1,0:T(8,128)(2,1)S(1)}, u32[]{:S(2)}, u32[]{:S(2)}) collective-permute-start(bf16[1024,128]{1,0:T(8,128)(2,1)} %bitcast.9), channel_id=1, source_target_pairs={{0,2},{1,3},{2,0},{3,1},{4,6},{5,7},{6,4},{7,5},{8,10},{9,11},{10,... | collective-permute-start | bytes 786440 | tf_op jit(solution)/shard_map/ppermute | solution.py:432
  26.1 1.3 prepare.1
  27.8 5.1 %collective-permute-done.4.refs_2_ = bf16[1024,128]{1,0:T(8,128)(2,1)S(1)} collective-permute-done((bf16[1024,128]{1,0:T(8,128)(2,1)}, bf16[1024,128]{1,0:T(8,128)(2,1)S(1)}, u32[]{:S(2)}, u32[]{:S(2)}) %collective-permute-start.4) | collective-permute-done | bytes 262176 | tf_op jit(solution)/shard_map/ppermute | solution.py:432
  32.9 2.9 %collective-permute-done.5.refs_3_ = bf16[1024,128]{1,0:T(8,128)(2,1)S(1)} collective-permute-done((bf16[1024,128]{1,0:T(8,128)(2,1)}, bf16[1024,128]{1,0:T(8,128)(2,1)S(1)}, u32[]{:S(2)}, u32[]{:S(2)}) %collective-permute-start.5) | collective-permute-done | bytes 262176 | tf_op jit(solution)/shard_map/ppermute | solution.py:432
  35.8 1.9 %collective-permute-done.3.refs_1_ = bf16[1024,128]{1,0:T(8,128)(2,1)S(1)} collective-permute-done((bf16[1024,128]{1,0:T(8,128)(2,1)}, bf16[1024,128]{1,0:T(8,128)(2,1)S(1)}, u32[]{:S(2)}, u32[]{:S(2)}) %collective-permute-start.3) | collective-permute-done | bytes 262176 | tf_op jit(solution)/shard_map/ppermute | solution.py:432
  37.7 2.6 %grad_hidden.1 = bf16[128,32,128]{2,1,0:T(8,128)(2,1)} custom-call(s32[1]{0:T(128)} %bitcast.me_ref, bf16[512,512]{1,0:T(8,128)(2,1)S(1)} %copy-done.10, bf16[1024,128]{1,0:T(8,128)(2,1)S(1)} %bitcast.39, bf16[1024,128]{1,0:T(8,128)(2,1)S(1)} %collective-permute-done.3.refs_1_, bf16[1024,128]{1,0:T(8,128)(2,1)S(1)} %collective-permute-done.4.refs_2_, ...), custom_call_target="tpu_custom_call" | custom-call | flops 1000 | bytes 1000 | tf_op jit(solution)/shard_map/grad_hidden/pallas_call | solution.py:141
  40.3 8.3 %all-to-all-start.1 = ((bf16[128,32,128]{2,1,0:T(8,128)(2,1)}), bf16[128,32,128]{2,1,0:T(8,128)(2,1)S(1)}, u32[]{:S(2)}, u32[]{:S(2)}) async-start(bf16[128,32,128]{2,1,0:T(8,128)(2,1)} %grad_hidden.1), calls=%async_computation.1 | async-start | bytes 2097152 | tf_op jit(solution)/shard_map/all_to_all | solution.py:421
  48.6 1.5 %convert_element_type.24.x_ref = f32[32,4,32,128]{3,2,1,0:T(8,128)S(1)} convert(f16[32,4,32,128]{3,2,1,0:T(8,128)(2,1)} %all-to-all-done) | non-fusion elementwise | flops 524288 | bytes 3145728 | tf_op jit(solution)/shard_map/convert_element_type | solution.py:487
  50.1 11.1 %forward.1 = (bf16[32,4,32,128]{3,2,1,0:T(8,128)(2,1)S(1)}, f32[4,32,4,8,128]{4,3,2,1,0:T(8,128)S(1)}) custom-call(f32[32,4,32,128]{3,2,1,0:T(8,128)S(1)} %convert_element_type.24.x_ref, s32[32,4,8,128]{3,2,1,0:T(8,128)S(1)} %get-tuple-element.24.rel_ref, f32[128]{0:T(128)S(1)} %reshape.67.t_ref), custom_call_target="tpu_custom_call" | custom-call | flops 1000 | bytes 1000 | tf_op jit(solution)/shard_map/forward/pallas_call | solution.py:213
  61.2 1.4 %copy-done.6 = f32[4,32,4,8,128]{4,3,2,1,0:T(8,128)} copy-done((f32[4,32,4,8,128]{4,3,2,1,0:T(8,128)}, f32[4,32,4,8,128]{4,3,2,1,0:T(8,128)S(1)}, u32[]{:S(2)}) %copy-start.6) | copy-done | bytes 2097176
  63.5 3.6 %all-to-all-done.1 = bf16[128,32,128]{2,1,0:T(8,128)(2,1)S(1)} async-done(((bf16[128,32,128]{2,1,0:T(8,128)(2,1)}), bf16[128,32,128]{2,1,0:T(8,128)(2,1)S(1)}, u32[]{:S(2)}, u32[]{:S(2)}) %all-to-all-start.1) | async-done | bytes 1048608 | tf_op jit(solution)/shard_map/all_to_all | solution.py:421
  67.2 6.1 %all-to-all-start.2 = ((bf16[128,32,128]{2,1,0:T(8,128)(2,1)}), bf16[128,32,128]{2,1,0:T(8,128)(2,1)S(1)}, u32[]{:S(2)}, u32[]{:S(2)}) async-start(bf16[128,32,128]{2,1,0:T(8,128)(2,1)} %bitcast.41), calls=%async_computation.2 | async-start | bytes 2097152 | tf_op jit(solution)/shard_map/all_to_all | solution.py:421
  73.3 2.4 %pad_maximum_fusion.held_ref = bf16[4,1024,128]{2,1,0:T(8,128)(2,1)} fusion(bf16[1,1024,128]{2,1,0:T(8,128)(2,1)} %bitcast.43, bf16[1,1024,128]{2,1,0:T(8,128)(2,1)} %bitcast.42, bf16[1,1024,128]{2,1,0:T(8,128)(2,1)} %bitcast.44, bf16[1,1024,128]{2,1,0:T(8,128)(2,1)S(1)} %bitcast.40), kind=kLoop, calls=%fused_computation.2 | loop fusion | flops 1572864 | bytes 2097152 | tf_op jit(solution)/shard_map/stack | solution.py:492
  76.7 10.9 %backward.1 = bf16[32,4,32,128]{3,2,1,0:T(8,128)(2,1)S(1)} custom-call(bf16[32,4,32,128]{3,2,1,0:T(8,128)(2,1)S(1)} %bitcast.38, f32[4,32,4,8,128]{4,3,2,1,0:T(8,128)S(1)} %copy-done.7, s32[32,4,8,128]{3,2,1,0:T(8,128)S(1)} %copy-done.9, f32[128]{0:T(128)S(1)} %reshape.67.t_ref), custom_call_target="tpu_custom_call" | custom-call | flops 1000 | bytes 1000 | tf_op jit(solution)/shard_map/backward/pallas_call | solution.py:285
  88.6 3.3 %all-to-all-done.2.hid_ref = bf16[128,32,128]{2,1,0:T(8,128)(2,1)S(1)} async-done(((bf16[128,32,128]{2,1,0:T(8,128)(2,1)}), bf16[128,32,128]{2,1,0:T(8,128)(2,1)S(1)}, u32[]{:S(2)}, u32[]{:S(2)}) %all-to-all-start.2) | async-done | bytes 1048608 | tf_op jit(solution)/shard_map/all_to_all | solution.py:421
  91.9 4.8 %all-to-all-start.3 = ((bf16[32,4,32,128]{3,2,1,0:T(8,128)(2,1)}), bf16[32,4,32,128]{3,2,1,0:T(8,128)(2,1)S(1)}, u32[]{:S(2)}, u32[]{:S(2)}) async-start(bf16[32,4,32,128]{3,2,1,0:T(8,128)(2,1)} %copy-done.4), calls=%async_computation.3 | async-start | bytes 2097152 | tf_op jit(solution)/shard_map/all_to_all | solution.py:421
  97.9 1.6 %weigh.1 = (f32[512,128]{1,0:T(8,128)S(1)}, bf16[512,128]{1,0:T(8,128)(2,1)S(1)}, bf16[512,128]{1,0:T(8,128)(2,1)S(1)}, bf16[512,128]{1,0:T(8,128)(2,1)S(1)}) custom-call(s32[1]{0:T(128)} %bitcast.me_ref, bf16[128,32,128]{2,1,0:T(8,128)(2,1)S(1)} %all-to-all-done.2.hid_ref, bf16[4,1024,128]{2,1,0:T(8,128)(2,1)S(1)} %copy-done.5), custom_call_target="tpu_custom_call" | custom-call | flops 1000 | bytes 1000 | tf_op jit(solution)/shard_map/weigh/pallas_call | solution.py:333
  99.6 1.3 collective-permute-start.12
  100.8 3.2 %collective-permute-start.13 = (bf16[512,128]{1,0:T(8,128)(2,1)S(1)}, bf16[512,128]{1,0:T(8,128)(2,1)S(1)}, u32[]{:S(2)}, u32[]{:S(2)}) collective-permute-start(bf16[512,128]{1,0:T(8,128)(2,1)S(1)} %get-tuple-element.41), channel_id=1, source_target_pairs={{0,2},{1,3},{2,0},{3,1},{4,6},{5,7},{6,4},{7,5},{8,10},{9,11},{10,... | collective-permute-start | bytes 393224 | tf_op jit(solution)/shard_map/ppermute | solution.py:432
  105.3 2.5 %mix.1 = (bf16[1024,128]{1,0:T(8,128)(2,1)S(1)}, bf16[1024,128]{1,0:T(8,128)(2,1)}, bf16[1024,128]{1,0:T(8,128)(2,1)}, bf16[1024,128]{1,0:T(8,128)(2,1)}) custom-call(s32[1]{0:T(128)} %bitcast.me_ref, bf16[128,32,128]{2,1,0:T(8,128)(2,1)S(1)} %all-to-all-done.2.hid_ref, bf16[512,512]{1,0:T(8,128)(2,1)S(1)} %copy-done.11), custom_call_target="tpu_custom_call" | custom-call | flops 1000 | bytes 1000 | tf_op jit(solution)/shard_map/mix/pallas_call | solution.py:359
  109.2 2.0 %collective-permute-start.8 = (bf16[1024,128]{1,0:T(8,128)(2,1)}, bf16[1024,128]{1,0:T(8,128)(2,1)}, u32[]{:S(2)}, u32[]{:S(2)}) collective-permute-start(bf16[1024,128]{1,0:T(8,128)(2,1)} %get-tuple-element.36), channel_id=1, source_target_pairs={{0,3},{1,0},{2,1},{3,2},{4,7},{5,4},{6,5},{7,6},{8,11},{9,8},{10,9... | collective-permute-start | bytes 786440 | tf_op jit(solution)/shard_map/ppermute | solution.py:432
  114.0 6.5 %all-to-all-start.4 = ((f32[32,16,128]{2,1,0:T(8,128)}), f32[32,16,128]{2,1,0:T(8,128)}, u32[]{:S(2)}, u32[]{:S(2)}) async-start(f32[32,16,128]{2,1,0:T(8,128)} %bitcast.46), calls=%async_computation.4 | async-start | bytes 524288 | tf_op jit(solution)/shard_map/all_to_all | solution.py:421
  120.5 1.8 %collective-permute-start.11 = (f32[32,128]{1,0:T(8,128)S(1)}, f32[32,128]{1,0:T(8,128)S(1)}, u32[]{:S(2)}, u32[]{:S(2)}) collective-permute-start(f32[32,128]{1,0:T(8,128)S(1)} %inner.1), channel_id=1, source_target_pairs={{0,3},{1,0},{2,1},{3,2},{4,7},{5,4},{6,5},{7,6},{8,11},{9,8},{10,9... | collective-permute-start | bytes 49160 | tf_op jit(solution)/shard_map/ppermute | solution.py:432
  123.3 1.3 %collective-permute-start.9 = (f32[32,128]{1,0:T(8,128)S(1)}, f32[32,128]{1,0:T(8,128)S(1)}, u32[]{:S(2)}, u32[]{:S(2)}) collective-permute-start(f32[32,128]{1,0:T(8,128)S(1)} %inner.1), channel_id=1, source_target_pairs={{0,1},{1,2},{2,3},{3,0},{4,5},{5,6},{6,7},{7,4},{8,9},{9,10},{10,1... | collective-permute-start | bytes 49160 | tf_op jit(solution)/shard_map/ppermute | solution.py:432
  124.7 2.3 %whole.1 = bf16[8,4,128,128]{3,2,1,0:T(8,128)(2,1)} custom-call(s32[1]{0:T(128)} %bitcast.me_ref, bf16[8,4,128,128]{3,2,1,0:T(8,128)(2,1)S(1)} %bitcast.36, bf16[1024,128]{1,0:T(8,128)(2,1)S(1)} %get-tuple-element.33.refs_0_, bf16[1024,128]{1,0:T(8,128)(2,1)} %collective-permute-done.6.refs_1_, bf16[1024,128]{1,0:T(8,128)(2,1)} %collective-permute-done.7.refs_2_, ...), custom_call_target="tpu_custom_call" | custom-call | flops 1000 | bytes 1000 | tf_op jit(solution)/shard_map/whole/pallas_call | solution.py:456
  128.3 2.6 %grad_in.1 = bf16[4096,128]{1,0:T(8,128)(2,1)} custom-call(bf16[32,4,32,128]{3,2,1,0:T(8,128)(2,1)S(1)} %all-to-all-done.3.v_ref, bf16[32,4,32,128]{3,2,1,0:T(8,128)(2,1)S(1)} %turn.1.xt_ref, bf16[4096,128]{1,0:T(8,128)(2,1)S(1)} %copy-done.3, f32[32,128]{1,0:T(8,128)S(1)} %get-tuple-element.46.inv_ref, f32[32,128]{1,0:T(8,128)S(1)} %add_multiply_fusion.mean_ref, ...), custom_call_target="tpu_custom_call" | custom-call | flops 1000 | bytes 1000 | tf_op jit(solution)/shard_map/grad_in/pallas_call | solution.py:408
  (74 shorter events, 18.7 us)
Async XLA Ops:
  2.5 7.3 %collective-permute-start.2 = (f32[32,128]{1,0:T(8,128)S(1)}, f32[32,128]{1,0:T(8,128)S(1)}, u32[]{:S(2)}, u32[]{:S(2)}) collective-permute-start(f32[32,128]{1,0:T(8,128)S(1)} %bitcast.50), channel_id=1, source_target_pairs={{0,3},{1,0},{2,1},{3,2},{4,7},{5,4},{6,5},{7,6},{8,11},{9,8},{10,9... | collective-permute-start | bytes 49160 | tf_op jit(solution)/shard_map/ppermute | solution.py:432
  6.6 5.2 %collective-permute-start.1 = (f32[32,128]{1,0:T(8,128)S(1)}, f32[32,128]{1,0:T(8,128)S(1)}, u32[]{:S(2)}, u32[]{:S(2)}) collective-permute-start(f32[32,128]{1,0:T(8,128)S(1)} %bitcast.51), channel_id=1, source_target_pairs={{0,2},{1,3},{2,0},{3,1},{4,6},{5,7},{6,4},{7,5},{8,10},{9,11},{10,... | collective-permute-start | bytes 49160 | tf_op jit(solution)/shard_map/ppermute | solution.py:432
  6.6 5.2 %collective-permute-start = (f32[32,128]{1,0:T(8,128)S(1)}, f32[32,128]{1,0:T(8,128)S(1)}, u32[]{:S(2)}, u32[]{:S(2)}) collective-permute-start(f32[32,128]{1,0:T(8,128)S(1)} %bitcast.52), channel_id=1, source_target_pairs={{0,1},{1,2},{2,3},{3,0},{4,5},{5,6},{6,7},{7,4},{8,9},{9,10},{10,1... | collective-permute-start | bytes 49160 | tf_op jit(solution)/shard_map/ppermute | solution.py:432
  11.9 9.2 %copy-start.2 = (bf16[4096,128]{1,0:T(8,128)(2,1)S(1)}, bf16[4096,128]{1,0:T(8,128)(2,1)}, u32[]{:S(2)}) copy-start(bf16[4096,128]{1,0:T(8,128)(2,1)} %cot_ref.1) | copy-start | bytes 3145732
  13.2 12.9 %copy-start.16 = (f32[15,2,128]{2,1,0:T(2,128)S(1)}, f32[15,2,128]{2,1,0:T(2,128)}, u32[]{:S(2)}) copy-start(f32[15,2,128]{2,1,0:T(2,128)} %low_ref.1) | copy-start | bytes 46084
  13.2 12.9 %copy-start.17 = (f32[15,2,128]{2,1,0:T(2,128)S(1)}, f32[15,2,128]{2,1,0:T(2,128)}, u32[]{:S(2)}) copy-start(f32[15,2,128]{2,1,0:T(2,128)} %high_ref.1) | copy-start | bytes 46084
  13.2 12.9 %copy-start.18 = (f32[16,128]{1,0:T(8,128)S(1)}, f32[16,128]{1,0:T(8,128)}, u32[]{:S(2)}) copy-start(f32[16,128]{1,0:T(8,128)} %level_ref.1) | copy-start | bytes 24580
  13.2 12.9 %copy-start.19 = (f32[128]{0:T(128)S(1)}, f32[128]{0:T(128)}, u32[]{:S(2)}) copy-start(f32[128]{0:T(128)} %gain_ref.3) | copy-start | bytes 1540
  13.2 12.9 %copy-start.20 = (s32[16]{0:T(128)S(1)}, s32[16]{0:T(128)}, u32[]{:S(2)}) copy-start(s32[16]{0:T(128)} %len_ref.1) | copy-start | bytes 196
  13.2 24.5 %copy-start.10 = (bf16[512,512]{1,0:T(8,128)(2,1)S(1)}, bf16[512,512]{1,0:T(8,128)(2,1)}, u32[]{:S(2)}) copy-start(bf16[512,512]{1,0:T(8,128)(2,1)} %mix_ref.3) | copy-start | bytes 1572868
  13.2 27.1 %all-to-all-start = ((f16[32,4,32,128]{3,2,1,0:T(8,128)(2,1)}), f16[32,4,32,128]{3,2,1,0:T(8,128)(2,1)}, u32[]{:S(2)}, u32[]{:S(2)}) async-start(f16[32,4,32,128]{3,2,1,0:T(8,128)(2,1)} %multiply_convert_fusion), calls=%async_computation | async-start | bytes 2097152 | tf_op jit(solution)/shard_map/all_to_all | solution.py:421
  22.0 10.9 %collective-permute-start.4 = (bf16[1024,128]{1,0:T(8,128)(2,1)}, bf16[1024,128]{1,0:T(8,128)(2,1)S(1)}, u32[]{:S(2)}, u32[]{:S(2)}) collective-permute-start(bf16[1024,128]{1,0:T(8,128)(2,1)} %bitcast.9), channel_id=1, source_target_pairs={{0,2},{1,3},{2,0},{3,1},{4,6},{5,7},{6,4},{7,5},{8,10},{9,11},{10,... | collective-permute-start | bytes 786440 | tf_op jit(solution)/shard_map/ppermute | solution.py:432
  24.0 11.8 %collective-permute-start.5 = (bf16[1024,128]{1,0:T(8,128)(2,1)}, bf16[1024,128]{1,0:T(8,128)(2,1)S(1)}, u32[]{:S(2)}, u32[]{:S(2)}) collective-permute-start(bf16[1024,128]{1,0:T(8,128)(2,1)} %bitcast.10), channel_id=1, source_target_pairs={{0,3},{1,0},{2,1},{3,2},{4,7},{5,4},{6,5},{7,6},{8,11},{9,8},{10,9... | collective-permute-start | bytes 786440 | tf_op jit(solution)/shard_map/ppermute | solution.py:432
  24.8 12.9 %collective-permute-start.3 = (bf16[1024,128]{1,0:T(8,128)(2,1)}, bf16[1024,128]{1,0:T(8,128)(2,1)S(1)}, u32[]{:S(2)}, u32[]{:S(2)}) collective-permute-start(bf16[1024,128]{1,0:T(8,128)(2,1)} %bitcast.8), channel_id=1, source_target_pairs={{0,1},{1,2},{2,3},{3,0},{4,5},{5,6},{6,7},{7,4},{8,9},{9,10},{10,1... | collective-permute-start | bytes 786440 | tf_op jit(solution)/shard_map/ppermute | solution.py:432
  27.4 22.7 %copy-start.8 = (s32[32,4,8,128]{3,2,1,0:T(8,128)}, s32[32,4,8,128]{3,2,1,0:T(8,128)S(1)}, u32[]{:S(2)}) copy-start(s32[32,4,8,128]{3,2,1,0:T(8,128)S(1)} %get-tuple-element.24.rel_ref) | copy-start | bytes 1572868
  32.9 7.4 %copy-start.13 = (bf16[1024,128]{1,0:T(8,128)(2,1)}, bf16[1024,128]{1,0:T(8,128)(2,1)S(1)}, u32[]{:S(2)}) copy-start(bf16[1024,128]{1,0:T(8,128)(2,1)S(1)} %collective-permute-done.4.refs_2_) | copy-start | bytes 786436
  40.3 26.9 %all-to-all-start.1 = ((bf16[128,32,128]{2,1,0:T(8,128)(2,1)}), bf16[128,32,128]{2,1,0:T(8,128)(2,1)S(1)}, u32[]{:S(2)}, u32[]{:S(2)}) async-start(bf16[128,32,128]{2,1,0:T(8,128)(2,1)} %grad_hidden.1), calls=%async_computation.1 | async-start | bytes 2097152 | tf_op jit(solution)/shard_map/all_to_all | solution.py:421
  67.2 24.7 %all-to-all-start.2 = ((bf16[128,32,128]{2,1,0:T(8,128)(2,1)}), bf16[128,32,128]{2,1,0:T(8,128)(2,1)S(1)}, u32[]{:S(2)}, u32[]{:S(2)}) async-start(bf16[128,32,128]{2,1,0:T(8,128)(2,1)} %bitcast.41), calls=%async_computation.2 | async-start | bytes 2097152 | tf_op jit(solution)/shard_map/all_to_all | solution.py:421
  91.9 21.1 %all-to-all-start.3 = ((bf16[32,4,32,128]{3,2,1,0:T(8,128)(2,1)}), bf16[32,4,32,128]{3,2,1,0:T(8,128)(2,1)S(1)}, u32[]{:S(2)}, u32[]{:S(2)}) async-start(bf16[32,4,32,128]{3,2,1,0:T(8,128)(2,1)} %copy-done.4), calls=%async_computation.3 | async-start | bytes 2097152 | tf_op jit(solution)/shard_map/all_to_all | solution.py:421
  97.9 7.3 %copy-start.11 = (bf16[512,512]{1,0:T(8,128)(2,1)S(1)}, bf16[512,512]{1,0:T(8,128)(2,1)}, u32[]{:S(2)}) copy-start(bf16[512,512]{1,0:T(8,128)(2,1)} %mix_ref.3) | copy-start | bytes 1572868
  99.6 9.6 %collective-permute-start.12 = (bf16[512,128]{1,0:T(8,128)(2,1)S(1)}, bf16[512,128]{1,0:T(8,128)(2,1)S(1)}, u32[]{:S(2)}, u32[]{:S(2)}) collective-permute-start(bf16[512,128]{1,0:T(8,128)(2,1)S(1)} %get-tuple-element.40), channel_id=1, source_target_pairs={{0,1},{1,2},{2,3},{3,0},{4,5},{5,6},{6,7},{7,4},{8,9},{9,10},{10,1... | collective-permute-start | bytes 393224 | tf_op jit(solution)/shard_map/ppermute | solution.py:432
  100.8 10.4 %collective-permute-start.13 = (bf16[512,128]{1,0:T(8,128)(2,1)S(1)}, bf16[512,128]{1,0:T(8,128)(2,1)S(1)}, u32[]{:S(2)}, u32[]{:S(2)}) collective-permute-start(bf16[512,128]{1,0:T(8,128)(2,1)S(1)} %get-tuple-element.41), channel_id=1, source_target_pairs={{0,2},{1,3},{2,0},{3,1},{4,6},{5,7},{6,4},{7,5},{8,10},{9,11},{10,... | collective-permute-start | bytes 393224 | tf_op jit(solution)/shard_map/ppermute | solution.py:432
  104.1 7.2 %collective-permute-start.14 = (bf16[512,128]{1,0:T(8,128)(2,1)S(1)}, bf16[512,128]{1,0:T(8,128)(2,1)S(1)}, u32[]{:S(2)}, u32[]{:S(2)}) collective-permute-start(bf16[512,128]{1,0:T(8,128)(2,1)S(1)} %get-tuple-element.42), channel_id=1, source_target_pairs={{0,3},{1,0},{2,1},{3,2},{4,7},{5,4},{6,5},{7,6},{8,11},{9,8},{10,9... | collective-permute-start | bytes 393224 | tf_op jit(solution)/shard_map/ppermute | solution.py:432
  107.7 16.9 %copy-start.1 = (bf16[4096,128]{1,0:T(8,128)(2,1)S(1)}, bf16[4096,128]{1,0:T(8,128)(2,1)}, u32[]{:S(2)}) copy-start(bf16[4096,128]{1,0:T(8,128)(2,1)} %x_ref.1) | copy-start | bytes 3145732
  107.7 15.6 %collective-permute-start.6 = (bf16[1024,128]{1,0:T(8,128)(2,1)}, bf16[1024,128]{1,0:T(8,128)(2,1)}, u32[]{:S(2)}, u32[]{:S(2)}) collective-permute-start(bf16[1024,128]{1,0:T(8,128)(2,1)} %get-tuple-element.34), channel_id=1, source_target_pairs={{0,1},{1,2},{2,3},{3,0},{4,5},{5,6},{6,7},{7,4},{8,9},{9,10},{10,1... | collective-permute-start | bytes 786440 | tf_op jit(solution)/shard_map/ppermute | solution.py:432
  108.6 16.1 %collective-permute-start.7 = (bf16[1024,128]{1,0:T(8,128)(2,1)}, bf16[1024,128]{1,0:T(8,128)(2,1)}, u32[]{:S(2)}, u32[]{:S(2)}) collective-permute-start(bf16[1024,128]{1,0:T(8,128)(2,1)} %get-tuple-element.35), channel_id=1, source_target_pairs={{0,2},{1,3},{2,0},{3,1},{4,6},{5,7},{6,4},{7,5},{8,10},{9,11},{10,... | collective-permute-start | bytes 786440 | tf_op jit(solution)/shard_map/ppermute | solution.py:432
  109.2 15.5 %collective-permute-start.8 = (bf16[1024,128]{1,0:T(8,128)(2,1)}, bf16[1024,128]{1,0:T(8,128)(2,1)}, u32[]{:S(2)}, u32[]{:S(2)}) collective-permute-start(bf16[1024,128]{1,0:T(8,128)(2,1)} %get-tuple-element.36), channel_id=1, source_target_pairs={{0,3},{1,0},{2,1},{3,2},{4,7},{5,4},{6,5},{7,6},{8,11},{9,8},{10,9... | collective-permute-start | bytes 786440 | tf_op jit(solution)/shard_map/ppermute | solution.py:432
  114.0 16.9 %all-to-all-start.4 = ((f32[32,16,128]{2,1,0:T(8,128)}), f32[32,16,128]{2,1,0:T(8,128)}, u32[]{:S(2)}, u32[]{:S(2)}) async-start(f32[32,16,128]{2,1,0:T(8,128)} %bitcast.46), calls=%async_computation.4 | async-start | bytes 524288 | tf_op jit(solution)/shard_map/all_to_all | solution.py:421
  120.5 7.8 %copy-start.3 = (bf16[4096,128]{1,0:T(8,128)(2,1)S(1)}, bf16[4096,128]{1,0:T(8,128)(2,1)}, u32[]{:S(2)}) copy-start(bf16[4096,128]{1,0:T(8,128)(2,1)} %cot_ref.1) | copy-start | bytes 3145732
  120.5 6.5 %collective-permute-start.11 = (f32[32,128]{1,0:T(8,128)S(1)}, f32[32,128]{1,0:T(8,128)S(1)}, u32[]{:S(2)}, u32[]{:S(2)}) collective-permute-start(f32[32,128]{1,0:T(8,128)S(1)} %inner.1), channel_id=1, source_target_pairs={{0,3},{1,0},{2,1},{3,2},{4,7},{5,4},{6,5},{7,6},{8,11},{9,8},{10,9... | collective-permute-start | bytes 49160 | tf_op jit(solution)/shard_map/ppermute | solution.py:432
  122.4 5.2 %collective-permute-start.10 = (f32[32,128]{1,0:T(8,128)S(1)}, f32[32,128]{1,0:T(8,128)S(1)}, u32[]{:S(2)}, u32[]{:S(2)}) collective-permute-start(f32[32,128]{1,0:T(8,128)S(1)} %inner.1), channel_id=1, source_target_pairs={{0,2},{1,3},{2,0},{3,1},{4,6},{5,7},{6,4},{7,5},{8,10},{9,11},{10,... | collective-permute-start | bytes 49160 | tf_op jit(solution)/shard_map/ppermute | solution.py:432
  123.3 5.0 %collective-permute-start.9 = (f32[32,128]{1,0:T(8,128)S(1)}, f32[32,128]{1,0:T(8,128)S(1)}, u32[]{:S(2)}, u32[]{:S(2)}) collective-permute-start(f32[32,128]{1,0:T(8,128)S(1)} %inner.1), channel_id=1, source_target_pairs={{0,1},{1,2},{2,3},{3,0},{4,5},{5,6},{6,7},{7,4},{8,9},{9,10},{10,1... | collective-permute-start | bytes 49160 | tf_op jit(solution)/shard_map/ppermute | solution.py:432
  (9 other events, 16.2 us)
where the time goes:
time: 133 us; the launch traced here: 132 us
  starting transfers between devices  56.3 us (42%)
  Pallas kernels  36.6 us (28%)
  waiting for transfers between devices  21.1 us (16%)
  other arithmetic  9.4 us (7%)
  local copies, waits for them, and re-layouts  8.12 us (6%)
    all_to_all x5, starting transfers between devices, exchange(): return lax.all_to_all(a, axes, 0, 0, tiled=True)  33.6 us
    ppermute x15, starting transfers between devices, turned(): lax.ppermute(a, 'ch', [(j, (j + by) % ZN) for j in range(ZN)])  22.7 us
    ppermute x15, waiting for transfers between devices, turned(): lax.ppermute(a, 'ch', [(j, (j + by) % ZN) for j in range(ZN)])  13.3 us
    pallas_call x1, Pallas kernels, forward(): pl.pallas_call(functools.partial(forward_kernel, FWD), out_shape=(jax.Sha...  11.1 us
    pallas_call x1, Pallas kernels, backward(): pl.pallas_call(functools.partial(backward_kernel, BWD), out_shape=jax.Sha...  10.9 us
    all_to_all x5, waiting for transfers between devices, exchange(): return lax.all_to_all(a, axes, 0, 0, tiled=True)  7.83 us
    unnamed x42, local copies, waits for them, and re-layouts  6.84 us
  transfers between devices with their start and end apart: 20, of which 9 were waited for; matrix products, arithmetic and copies ran while one was open for 4% of the time, Pallas kernels for 28%

commit v1 on v0

--- a/solution.py
+++ b/solution.py
@@ -119,18 +119,21 @@
 
 def grad_hidden_kernel(me_ref, mix_ref, *refs):
     cot_refs, (out_ref, scr) = refs[:ZN], refs[ZN:]
-    for m in range(8):
-        acc = None
-        for k in range(ZN):
-            c = (me_ref[0] + ZN - k) % ZN
-            part = lax.dot_general(
-                mix_ref[:, pl.ds(pl.multiple_of(c * LANES, LANES), LANES)],
-                cot_refs[k][m * LANES : (m + 1) * LANES, :],
-                (((1,), (1,)), ((), ())),
-                preferred_element_type=F32,
-            )
-            acc = part if acc is None else acc + part
-        scr[m * (512 + GAP) : m * (512 + GAP) + 512, :] = acc
+    columns = [
+        pl.ds(pl.multiple_of((me_ref[0] + ZN - k) % ZN * LANES, LANES), LANES) for k in range(ZN)
+    ]
+    mixing = jnp.concatenate([mix_ref[:, column] for column in columns], axis=1)
+    for m in range(0, 8, 2):
+        rows = [cot_refs[k][m * LANES : (m + 2) * LANES, :] for k in range(ZN)]
+        part = lax.dot_general(
+            mixing,
+            jnp.concatenate(rows, axis=1),
+            (((1,), (1,)), ((), ())),
+            preferred_element_type=F32,
+        )
+        for n in range(2):
+            at = (m + n) * (512 + GAP)
+            scr[at : at + 512, :] = part[:, n * LANES : (n + 1) * LANES]
     for g in range(SEQ):
         for c in range(ZN):
             rows = [scr[pl.ds(c * LANES + i * SEQ + g, 8, stride=512 + GAP), :] for i in range(NCH)]
@@ -318,14 +321,14 @@
     wg_refs, (scr, acc) = refs[:ZN], refs[ZN:]
     for m, at, h in hidden_tiles(hid_ref, scr):
         hb = h.astype(BF16)
-        for k in range(ZN):
-            part = jnp.dot(hb, held_ref[k, at], preferred_element_type=F32)
-            acc[k] = part if m == 0 else acc[k] + part
+        rows = jnp.concatenate([held_ref[k, at] for k in range(ZN)], axis=1)
+        part = jnp.dot(hb, rows, preferred_element_type=F32)
+        acc[...] = part if m == 0 else acc[...] + part
     for n in range(ZN):
         row = pl.multiple_of((me_ref[0] + n) % ZN * LANES, LANES)
         for k in range(ZN):
             column = pl.multiple_of((me_ref[0] + ZN - k) % ZN * LANES, LANES)
-            t = acc[k, pl.ds(row, LANES), :].T
+            t = acc[pl.ds(row, LANES), k * LANES : (k + 1) * LANES].T
             wg_refs[n][pl.ds(column, LANES), :] = t.astype(wg_refs[n].dtype)
 
 
@@ -337,7 +340,7 @@
         out_specs=(vspec(),) * ZN,
         scratch_shapes=[
             VMEM((SEQ * (LANES + GAP), LANES), F32),
-            VMEM((ZN, 512, LANES), F32),
+            VMEM((512, 512), F32),
         ],
         compiler_params=params(),
         cost_estimate=cost(),
@@ -347,12 +350,14 @@
 
 def mix_kernel(me_ref, hid_ref, mix_ref, *refs):
     out_refs, scr = refs[:ZN], refs[ZN]
+    columns = [
+        pl.ds(pl.multiple_of((me_ref[0] + n) % ZN * LANES, LANES), LANES) for n in range(ZN)
+    ]
+    mixing = jnp.concatenate([mix_ref[:, column] for column in columns], axis=1)
     for m, at, h in hidden_tiles(hid_ref, scr):
-        ht = h.T.astype(BF16)
+        mixed = jnp.dot(h.T.astype(BF16), mixing, preferred_element_type=F32)
         for n in range(ZN):
-            column = pl.ds(pl.multiple_of((me_ref[0] + n) % ZN * LANES, LANES), LANES)
-            part = jnp.dot(ht, mix_ref[:, column], preferred_element_type=F32)
-            out_refs[n][at, :] = part.astype(BF16)
+            out_refs[n][at, :] = mixed[:, n * LANES : (n + 1) * LANES].astype(BF16)
 
 
 def mix(me, hid, mixing):
@@ -496,7 +501,7 @@
     shares = weigh(place, hid_rows, held)
     own_first = shares[0]
     shares = [turned(shares[n], n).astype(F32) for n in range(ZN)]
-    wg = shares[0] + shares[1] + shares[2] + shares[3]
+    wg = (shares[0] + shares[1] + shares[2] + shares[3]) / math.sqrt(bases)
     mixed = mix(after(place, own_first), hid_rows, mixing)
     parts = [turned(mixed[n], n) for n in range(ZN)]
     own = inner(v, xt, norm_gain)
@@ -504,7 +509,7 @@
     others = [turned(own, k) for k in range(1, ZN)]
     mean = (own + others[0] + others[1] + others[2]) / full
     grad_in = grad_in_of(v, xt, cotangent, inv, mean, norm_gain)
-    weight_grad = jnp.sum(after(wg, grad_in), axis=0).T / math.sqrt(bases)
+    weight_grad = jnp.sum(after(wg, grad_in), axis=0).T
     layer_out = whole_of(tokens, parts, place)
     return (layer_out, grad_in, weight_grad)
 

time: 133 us -> 133 us (level)
  transfers between devices with their start and end apart: 20 -> 20, of which waited for: 9 -> 10; matrix products, arithmetic and copies ran while one was open for 4% -> 4% of each run, Pallas kernels for 28% -> 27%
where the time goes in v1:
time: 133 us; the launch traced here: 132 us
  starting transfers between devices  55.4 us (42%)
  Pallas kernels  35.4 us (27%)
  waiting for transfers between devices  22.3 us (17%)
  other arithmetic  9.39 us (7%)
  local copies, waits for them, and re-layouts  8.12 us (6%)
    all_to_all x5, starting transfers between devices, exchange(): return lax.all_to_all(a, axes, 0, 0, tiled=True)  33.3 us
    ppermute x15, starting transfers between devices, turned(): lax.ppermute(a, 'ch', [(j, (j + by) % ZN) for j in range(ZN)])  22.1 us
    ppermute x15, waiting for transfers between devices, turned(): lax.ppermute(a, 'ch', [(j, (j + by) % ZN) for j in range(ZN)])  14.2 us
    pallas_call x1, Pallas kernels, forward(): pl.pallas_call(functools.partial(forward_kernel, FWD), out_shape=(jax.Sha...  11.1 us
    pallas_call x1, Pallas kernels, backward(): pl.pallas_call(functools.partial(backward_kernel, BWD), out_shape=jax.Sha...  10.9 us
    all_to_all x5, waiting for transfers between devices, exchange(): return lax.all_to_all(a, axes, 0, 0, tiled=True)  8.09 us
    unnamed x42, local copies, waits for them, and re-layouts  6.84 us
  transfers between devices with their start and end apart: 20, of which 10 were waited for; matrix products, arithmetic and copies ran while one was open for 4% of the time, Pallas kernels for 27%

profile of v1, /device:TPU:2, one launch (start us, length us, event | category | flops | bytes accessed | tf_op | source)
XLA Modules:
  0.0 131.7 jit_solution(859596972425418972)
XLA Ops:
  0.6 1.8 %multiply_reduce_fusion = f32[4096]{0:T(1024)S(1)} fusion(bf16[4096,128]{1,0:T(8,128)(2,1)} %x_ref.1), kind=kLoop, calls=%fused_computation.1 | loop fusion | flops 1568768 | bytes 1064960 | tf_op jit(solution)/shard_map/reduce_sum | solution.py:486
  2.5 4.1 %collective-permute-start.2 = (f32[32,128]{1,0:T(8,128)S(1)}, f32[32,128]{1,0:T(8,128)S(1)}, u32[]{:S(2)}, u32[]{:S(2)}) collective-permute-start(f32[32,128]{1,0:T(8,128)S(1)} %bitcast.49), channel_id=1, source_target_pairs={{0,3},{1,0},{2,1},{3,2},{4,7},{5,4},{6,5},{7,6},{8,11},{9,8},{10,9... | collective-permute-start | bytes 49160 | tf_op jit(solution)/shard_map/ppermute | solution.py:437
  6.6 1.3 collective-permute-start
  9.7 2.1 %collective-permute-done.1 = f32[32,128]{1,0:T(8,128)S(1)} collective-permute-done((f32[32,128]{1,0:T(8,128)S(1)}, f32[32,128]{1,0:T(8,128)S(1)}, u32[]{:S(2)}, u32[]{:S(2)}) %collective-permute-start.1) | collective-permute-done | bytes 16416 | tf_op jit(solution)/shard_map/ppermute | solution.py:437
  11.9 1.3 multiply_convert_fusion
  13.2 7.8 %all-to-all-start = ((f16[32,4,32,128]{3,2,1,0:T(8,128)(2,1)}), f16[32,4,32,128]{3,2,1,0:T(8,128)(2,1)}, u32[]{:S(2)}, u32[]{:S(2)}) async-start(f16[32,4,32,128]{3,2,1,0:T(8,128)(2,1)} %multiply_convert_fusion), calls=%async_computation | async-start | bytes 2097152 | tf_op jit(solution)/shard_map/all_to_all | solution.py:426
  22.0 2.0 %collective-permute-start.4 = (bf16[1024,128]{1,0:T(8,128)(2,1)}, bf16[1024,128]{1,0:T(8,128)(2,1)S(1)}, u32[]{:S(2)}, u32[]{:S(2)}) collective-permute-start(bf16[1024,128]{1,0:T(8,128)(2,1)} %bitcast.9), channel_id=1, source_target_pairs={{0,2},{1,3},{2,0},{3,1},{4,6},{5,7},{6,4},{7,5},{8,10},{9,11},{10,... | collective-permute-start | bytes 786440 | tf_op jit(solution)/shard_map/ppermute | solution.py:437
  26.1 1.3 %prepare.1 = (s32[32,4,8,128]{3,2,1,0:T(8,128)S(1)}, f32[32,128]{1,0:T(8,128)S(1)}) custom-call(s32[16]{0:T(128)S(1)} %copy-done.20, f32[15,2,128]{2,1,0:T(2,128)S(1)} %copy-done.16, f32[15,2,128]{2,1,0:T(2,128)S(1)} %copy-done.17, f32[16,128]{1,0:T(8,128)S(1)} %copy-done.18, f32[1,128]{1,0:T(1,128)S(1)} %bitcast.44), custom_call_target="tpu_custom_call" | custom-call | flops 1000 | bytes 1000 | tf_op jit(solution)/shard_map/prepare/pallas_call | solution.py:106
  27.8 5.1 %collective-permute-done.4.refs_2_ = bf16[1024,128]{1,0:T(8,128)(2,1)S(1)} collective-permute-done((bf16[1024,128]{1,0:T(8,128)(2,1)}, bf16[1024,128]{1,0:T(8,128)(2,1)S(1)}, u32[]{:S(2)}, u32[]{:S(2)}) %collective-permute-start.4) | collective-permute-done | bytes 262176 | tf_op jit(solution)/shard_map/ppermute | solution.py:437
  32.9 2.9 %collective-permute-done.5.refs_3_ = bf16[1024,128]{1,0:T(8,128)(2,1)S(1)} collective-permute-done((bf16[1024,128]{1,0:T(8,128)(2,1)}, bf16[1024,128]{1,0:T(8,128)(2,1)S(1)}, u32[]{:S(2)}, u32[]{:S(2)}) %collective-permute-start.5) | collective-permute-done | bytes 262176 | tf_op jit(solution)/shard_map/ppermute | solution.py:437
  35.8 1.9 %collective-permute-done.3.refs_1_ = bf16[1024,128]{1,0:T(8,128)(2,1)S(1)} collective-permute-done((bf16[1024,128]{1,0:T(8,128)(2,1)}, bf16[1024,128]{1,0:T(8,128)(2,1)S(1)}, u32[]{:S(2)}, u32[]{:S(2)}) %collective-permute-start.3) | collective-permute-done | bytes 262176 | tf_op jit(solution)/shard_map/ppermute | solution.py:437
  37.7 2.0 %grad_hidden.1 = bf16[128,32,128]{2,1,0:T(8,128)(2,1)} custom-call(s32[1]{0:T(128)} %bitcast.me_ref, bf16[512,512]{1,0:T(8,128)(2,1)S(1)} %copy-done.10, bf16[1024,128]{1,0:T(8,128)(2,1)S(1)} %bitcast.38, bf16[1024,128]{1,0:T(8,128)(2,1)S(1)} %collective-permute-done.3.refs_1_, bf16[1024,128]{1,0:T(8,128)(2,1)S(1)} %collective-permute-done.4.refs_2_, ...), custom_call_target="tpu_custom_call" | custom-call | flops 1000 | bytes 1000 | tf_op jit(solution)/shard_map/grad_hidden/pallas_call | solution.py:144
  39.7 8.3 %all-to-all-start.1 = ((bf16[128,32,128]{2,1,0:T(8,128)(2,1)}), bf16[128,32,128]{2,1,0:T(8,128)(2,1)S(1)}, u32[]{:S(2)}, u32[]{:S(2)}) async-start(bf16[128,32,128]{2,1,0:T(8,128)(2,1)} %grad_hidden.1), calls=%async_computation.1 | async-start | bytes 2097152 | tf_op jit(solution)/shard_map/all_to_all | solution.py:426
  48.0 1.5 %convert_element_type.24.x_ref = f32[32,4,32,128]{3,2,1,0:T(8,128)S(1)} convert(f16[32,4,32,128]{3,2,1,0:T(8,128)(2,1)} %all-to-all-done) | non-fusion elementwise | flops 524288 | bytes 3145728 | tf_op jit(solution)/shard_map/convert_element_type | solution.py:492
  49.5 11.1 %forward.1 = (bf16[32,4,32,128]{3,2,1,0:T(8,128)(2,1)S(1)}, f32[4,32,4,8,128]{4,3,2,1,0:T(8,128)S(1)}) custom-call(f32[32,4,32,128]{3,2,1,0:T(8,128)S(1)} %convert_element_type.24.x_ref, s32[32,4,8,128]{3,2,1,0:T(8,128)S(1)} %get-tuple-element.24.rel_ref, f32[128]{0:T(128)S(1)} %reshape.67.t_ref), custom_call_target="tpu_custom_call" | custom-call | flops 1000 | bytes 1000 | tf_op jit(solution)/shard_map/forward/pallas_call | solution.py:216
  60.6 1.4 %copy-done.6 = f32[4,32,4,8,128]{4,3,2,1,0:T(8,128)} copy-done((f32[4,32,4,8,128]{4,3,2,1,0:T(8,128)}, f32[4,32,4,8,128]{4,3,2,1,0:T(8,128)S(1)}, u32[]{:S(2)}) %copy-start.6) | copy-done | bytes 2097176
  62.9 3.6 %all-to-all-done.1 = bf16[128,32,128]{2,1,0:T(8,128)(2,1)S(1)} async-done(((bf16[128,32,128]{2,1,0:T(8,128)(2,1)}), bf16[128,32,128]{2,1,0:T(8,128)(2,1)S(1)}, u32[]{:S(2)}, u32[]{:S(2)}) %all-to-all-start.1) | async-done | bytes 1048608 | tf_op jit(solution)/shard_map/all_to_all | solution.py:426
  66.6 6.1 %all-to-all-start.2 = ((bf16[128,32,128]{2,1,0:T(8,128)(2,1)}), bf16[128,32,128]{2,1,0:T(8,128)(2,1)S(1)}, u32[]{:S(2)}, u32[]{:S(2)}) async-start(bf16[128,32,128]{2,1,0:T(8,128)(2,1)} %bitcast.40), calls=%async_computation.2 | async-start | bytes 2097152 | tf_op jit(solution)/shard_map/all_to_all | solution.py:426
  72.7 2.4 %pad_maximum_fusion.held_ref = bf16[4,1024,128]{2,1,0:T(8,128)(2,1)} fusion(bf16[1,1024,128]{2,1,0:T(8,128)(2,1)} %bitcast.42, bf16[1,1024,128]{2,1,0:T(8,128)(2,1)} %bitcast.41, bf16[1,1024,128]{2,1,0:T(8,128)(2,1)} %bitcast.43, bf16[1,1024,128]{2,1,0:T(8,128)(2,1)S(1)} %bitcast.39), kind=kLoop, calls=%fused_computation.2 | loop fusion | flops 1572864 | bytes 2097152 | tf_op jit(solution)/shard_map/stack | solution.py:497
  76.1 10.9 %backward.1 = bf16[32,4,32,128]{3,2,1,0:T(8,128)(2,1)S(1)} custom-call(bf16[32,4,32,128]{3,2,1,0:T(8,128)(2,1)S(1)} %bitcast.37, f32[4,32,4,8,128]{4,3,2,1,0:T(8,128)S(1)} %copy-done.7, s32[32,4,8,128]{3,2,1,0:T(8,128)S(1)} %copy-done.9, f32[128]{0:T(128)S(1)} %reshape.67.t_ref), custom_call_target="tpu_custom_call" | custom-call | flops 1000 | bytes 1000 | tf_op jit(solution)/shard_map/backward/pallas_call | solution.py:288
  88.0 3.3 %all-to-all-done.2.hid_ref = bf16[128,32,128]{2,1,0:T(8,128)(2,1)S(1)} async-done(((bf16[128,32,128]{2,1,0:T(8,128)(2,1)}), bf16[128,32,128]{2,1,0:T(8,128)(2,1)S(1)}, u32[]{:S(2)}, u32[]{:S(2)}) %all-to-all-start.2) | async-done | bytes 1048608 | tf_op jit(solution)/shard_map/all_to_all | solution.py:426
  91.3 4.8 %all-to-all-start.3 = ((bf16[32,4,32,128]{3,2,1,0:T(8,128)(2,1)}), bf16[32,4,32,128]{3,2,1,0:T(8,128)(2,1)S(1)}, u32[]{:S(2)}, u32[]{:S(2)}) async-start(bf16[32,4,32,128]{3,2,1,0:T(8,128)(2,1)} %copy-done.4), calls=%async_computation.3 | async-start | bytes 2097152 | tf_op jit(solution)/shard_map/all_to_all | solution.py:426
  97.3 1.6 %weigh.1 = (f32[512,128]{1,0:T(8,128)S(1)}, bf16[512,128]{1,0:T(8,128)(2,1)S(1)}, bf16[512,128]{1,0:T(8,128)(2,1)S(1)}, bf16[512,128]{1,0:T(8,128)(2,1)S(1)}) custom-call(s32[1]{0:T(128)} %bitcast.me_ref, bf16[128,32,128]{2,1,0:T(8,128)(2,1)S(1)} %all-to-all-done.2.hid_ref, bf16[4,1024,128]{2,1,0:T(8,128)(2,1)S(1)} %copy-done.5), custom_call_target="tpu_custom_call" | custom-call | flops 1000 | bytes 1000 | tf_op jit(solution)/shard_map/weigh/pallas_call | solution.py:336
  100.1 3.2 %collective-permute-start.13 = (bf16[512,128]{1,0:T(8,128)(2,1)S(1)}, bf16[512,128]{1,0:T(8,128)(2,1)S(1)}, u32[]{:S(2)}, u32[]{:S(2)}) collective-permute-start(bf16[512,128]{1,0:T(8,128)(2,1)S(1)} %get-tuple-element.41), channel_id=1, source_target_pairs={{0,2},{1,3},{2,0},{3,1},{4,6},{5,7},{6,4},{7,5},{8,10},{9,11},{10,... | collective-permute-start | bytes 393224 | tf_op jit(solution)/shard_map/ppermute | solution.py:437
  104.5 2.0 %mix.1 = (bf16[1024,128]{1,0:T(8,128)(2,1)S(1)}, bf16[1024,128]{1,0:T(8,128)(2,1)}, bf16[1024,128]{1,0:T(8,128)(2,1)}, bf16[1024,128]{1,0:T(8,128)(2,1)}) custom-call(s32[1]{0:T(128)} %bitcast.me_ref, bf16[128,32,128]{2,1,0:T(8,128)(2,1)S(1)} %all-to-all-done.2.hid_ref, bf16[512,512]{1,0:T(8,128)(2,1)S(1)} %copy-done.11), custom_call_target="tpu_custom_call" | custom-call | flops 1000 | bytes 1000 | tf_op jit(solution)/shard_map/mix/pallas_call | solution.py:364
  107.9 2.0 %collective-permute-start.8 = (bf16[1024,128]{1,0:T(8,128)(2,1)}, bf16[1024,128]{1,0:T(8,128)(2,1)}, u32[]{:S(2)}, u32[]{:S(2)}) collective-permute-start(bf16[1024,128]{1,0:T(8,128)(2,1)} %get-tuple-element.36), channel_id=1, source_target_pairs={{0,3},{1,0},{2,1},{3,2},{4,7},{5,4},{6,5},{7,6},{8,11},{9,8},{10,9... | collective-permute-start | bytes 786440 | tf_op jit(solution)/shard_map/ppermute | solution.py:437
  113.4 6.3 %all-to-all-start.4 = ((f32[32,16,128]{2,1,0:T(8,128)}), f32[32,16,128]{2,1,0:T(8,128)}, u32[]{:S(2)}, u32[]{:S(2)}) async-start(f32[32,16,128]{2,1,0:T(8,128)} %bitcast.45), calls=%async_computation.4 | async-start | bytes 524288 | tf_op jit(solution)/shard_map/all_to_all | solution.py:426
  119.7 2.1 %collective-permute-start.11 = (f32[32,128]{1,0:T(8,128)S(1)}, f32[32,128]{1,0:T(8,128)S(1)}, u32[]{:S(2)}, u32[]{:S(2)}) collective-permute-start(f32[32,128]{1,0:T(8,128)S(1)} %inner.1), channel_id=1, source_target_pairs={{0,3},{1,0},{2,1},{3,2},{4,7},{5,4},{6,5},{7,6},{8,11},{9,8},{10,9... | collective-permute-start | bytes 49160 | tf_op jit(solution)/shard_map/ppermute | solution.py:437
  123.4 2.3 %whole.1 = bf16[8,4,128,128]{3,2,1,0:T(8,128)(2,1)} custom-call(s32[1]{0:T(128)} %bitcast.me_ref, bf16[8,4,128,128]{3,2,1,0:T(8,128)(2,1)S(1)} %bitcast.35, bf16[1024,128]{1,0:T(8,128)(2,1)S(1)} %get-tuple-element.33.refs_0_, bf16[1024,128]{1,0:T(8,128)(2,1)} %collective-permute-done.6.refs_1_, bf16[1024,128]{1,0:T(8,128)(2,1)} %collective-permute-done.7.refs_2_, ...), custom_call_target="tpu_custom_call" | custom-call | flops 1000 | bytes 1000 | tf_op jit(solution)/shard_map/whole/pallas_call | solution.py:461
  125.7 1.3 collective-permute-done.10
  127.5 2.6 %grad_in.1 = bf16[4096,128]{1,0:T(8,128)(2,1)} custom-call(bf16[32,4,32,128]{3,2,1,0:T(8,128)(2,1)S(1)} %all-to-all-done.3.v_ref, bf16[32,4,32,128]{3,2,1,0:T(8,128)(2,1)S(1)} %turn.1.xt_ref, bf16[4096,128]{1,0:T(8,128)(2,1)S(1)} %copy-done.3, f32[32,128]{1,0:T(8,128)S(1)} %get-tuple-element.46.inv_ref, f32[32,128]{1,0:T(8,128)S(1)} %add_multiply_fusion.1.mean_ref, ...), custom_call_target="tpu_custom_call" | custom-call | flops 1000 | bytes 1000 | tf_op jit(solution)/shard_map/grad_in/pallas_call | solution.py:413
  130.1 1.6 %reduce_sum.19 = f32[16,128]{1,0:T(8,128)} reduce(f32[32,16,128]{2,1,0:T(8,128)} %all-to-all-done.4, f32[]{:T(128)} %constant.54.clone.1), dimensions={0}, to_apply=%region_1.2 | reduce | flops 63488 | bytes 270340 | tf_op jit(solution)/shard_map/reduce_sum | solution.py:512
  (73 shorter events, 18.7 us)
Async XLA Ops:
  2.5 7.3 %collective-permute-start.2 = (f32[32,128]{1,0:T(8,128)S(1)}, f32[32,128]{1,0:T(8,128)S(1)}, u32[]{:S(2)}, u32[]{:S(2)}) collective-permute-start(f32[32,128]{1,0:T(8,128)S(1)} %bitcast.49), channel_id=1, source_target_pairs={{0,3},{1,0},{2,1},{3,2},{4,7},{5,4},{6,5},{7,6},{8,11},{9,8},{10,9... | collective-permute-start | bytes 49160 | tf_op jit(solution)/shard_map/ppermute | solution.py:437
  6.6 5.2 %collective-permute-start.1 = (f32[32,128]{1,0:T(8,128)S(1)}, f32[32,128]{1,0:T(8,128)S(1)}, u32[]{:S(2)}, u32[]{:S(2)}) collective-permute-start(f32[32,128]{1,0:T(8,128)S(1)} %bitcast.50), channel_id=1, source_target_pairs={{0,2},{1,3},{2,0},{3,1},{4,6},{5,7},{6,4},{7,5},{8,10},{9,11},{10,... | collective-permute-start | bytes 49160 | tf_op jit(solution)/shard_map/ppermute | solution.py:437
  6.6 5.2 %collective-permute-start = (f32[32,128]{1,0:T(8,128)S(1)}, f32[32,128]{1,0:T(8,128)S(1)}, u32[]{:S(2)}, u32[]{:S(2)}) collective-permute-start(f32[32,128]{1,0:T(8,128)S(1)} %bitcast.51), channel_id=1, source_target_pairs={{0,1},{1,2},{2,3},{3,0},{4,5},{5,6},{6,7},{7,4},{8,9},{9,10},{10,1... | collective-permute-start | bytes 49160 | tf_op jit(solution)/shard_map/ppermute | solution.py:437
  11.9 9.2 %copy-start.2 = (bf16[4096,128]{1,0:T(8,128)(2,1)S(1)}, bf16[4096,128]{1,0:T(8,128)(2,1)}, u32[]{:S(2)}) copy-start(bf16[4096,128]{1,0:T(8,128)(2,1)} %cot_ref.1) | copy-start | bytes 3145732
  13.2 12.9 %copy-start.16 = (f32[15,2,128]{2,1,0:T(2,128)S(1)}, f32[15,2,128]{2,1,0:T(2,128)}, u32[]{:S(2)}) copy-start(f32[15,2,128]{2,1,0:T(2,128)} %low_ref.1) | copy-start | bytes 46084
  13.2 12.9 %copy-start.17 = (f32[15,2,128]{2,1,0:T(2,128)S(1)}, f32[15,2,128]{2,1,0:T(2,128)}, u32[]{:S(2)}) copy-start(f32[15,2,128]{2,1,0:T(2,128)} %high_ref.1) | copy-start | bytes 46084
  13.2 12.9 %copy-start.18 = (f32[16,128]{1,0:T(8,128)S(1)}, f32[16,128]{1,0:T(8,128)}, u32[]{:S(2)}) copy-start(f32[16,128]{1,0:T(8,128)} %level_ref.1) | copy-start | bytes 24580
  13.2 12.9 %copy-start.19 = (f32[128]{0:T(128)S(1)}, f32[128]{0:T(128)}, u32[]{:S(2)}) copy-start(f32[128]{0:T(128)} %gain_ref.3) | copy-start | bytes 1540
  13.2 12.9 %copy-start.20 = (s32[16]{0:T(128)S(1)}, s32[16]{0:T(128)}, u32[]{:S(2)}) copy-start(s32[16]{0:T(128)} %len_ref.1) | copy-start | bytes 196
  13.2 24.5 %copy-start.10 = (bf16[512,512]{1,0:T(8,128)(2,1)S(1)}, bf16[512,512]{1,0:T(8,128)(2,1)}, u32[]{:S(2)}) copy-start(bf16[512,512]{1,0:T(8,128)(2,1)} %mix_ref.3) | copy-start | bytes 1572868
  13.2 26.4 %all-to-all-start = ((f16[32,4,32,128]{3,2,1,0:T(8,128)(2,1)}), f16[32,4,32,128]{3,2,1,0:T(8,128)(2,1)}, u32[]{:S(2)}, u32[]{:S(2)}) async-start(f16[32,4,32,128]{3,2,1,0:T(8,128)(2,1)} %multiply_convert_fusion), calls=%async_computation | async-start | bytes 2097152 | tf_op jit(solution)/shard_map/all_to_all | solution.py:426
  22.0 10.9 %collective-permute-start.4 = (bf16[1024,128]{1,0:T(8,128)(2,1)}, bf16[1024,128]{1,0:T(8,128)(2,1)S(1)}, u32[]{:S(2)}, u32[]{:S(2)}) collective-permute-start(bf16[1024,128]{1,0:T(8,128)(2,1)} %bitcast.9), channel_id=1, source_target_pairs={{0,2},{1,3},{2,0},{3,1},{4,6},{5,7},{6,4},{7,5},{8,10},{9,11},{10,... | collective-permute-start | bytes 786440 | tf_op jit(solution)/shard_map/ppermute | solution.py:437
  24.0 11.8 %collective-permute-start.5 = (bf16[1024,128]{1,0:T(8,128)(2,1)}, bf16[1024,128]{1,0:T(8,128)(2,1)S(1)}, u32[]{:S(2)}, u32[]{:S(2)}) collective-permute-start(bf16[1024,128]{1,0:T(8,128)(2,1)} %bitcast.10), channel_id=1, source_target_pairs={{0,3},{1,0},{2,1},{3,2},{4,7},{5,4},{6,5},{7,6},{8,11},{9,8},{10,9... | collective-permute-start | bytes 786440 | tf_op jit(solution)/shard_map/ppermute | solution.py:437
  24.9 12.9 %collective-permute-start.3 = (bf16[1024,128]{1,0:T(8,128)(2,1)}, bf16[1024,128]{1,0:T(8,128)(2,1)S(1)}, u32[]{:S(2)}, u32[]{:S(2)}) collective-permute-start(bf16[1024,128]{1,0:T(8,128)(2,1)} %bitcast.8), channel_id=1, source_target_pairs={{0,1},{1,2},{2,3},{3,0},{4,5},{5,6},{6,7},{7,4},{8,9},{9,10},{10,1... | collective-permute-start | bytes 786440 | tf_op jit(solution)/shard_map/ppermute | solution.py:437
  27.4 22.1 %copy-start.8 = (s32[32,4,8,128]{3,2,1,0:T(8,128)}, s32[32,4,8,128]{3,2,1,0:T(8,128)S(1)}, u32[]{:S(2)}) copy-start(s32[32,4,8,128]{3,2,1,0:T(8,128)S(1)} %get-tuple-element.24.rel_ref) | copy-start | bytes 1572868
  32.9 6.7 %copy-start.13 = (bf16[1024,128]{1,0:T(8,128)(2,1)}, bf16[1024,128]{1,0:T(8,128)(2,1)S(1)}, u32[]{:S(2)}) copy-start(bf16[1024,128]{1,0:T(8,128)(2,1)S(1)} %collective-permute-done.4.refs_2_) | copy-start | bytes 786436
  39.7 26.9 %all-to-all-start.1 = ((bf16[128,32,128]{2,1,0:T(8,128)(2,1)}), bf16[128,32,128]{2,1,0:T(8,128)(2,1)S(1)}, u32[]{:S(2)}, u32[]{:S(2)}) async-start(bf16[128,32,128]{2,1,0:T(8,128)(2,1)} %grad_hidden.1), calls=%async_computation.1 | async-start | bytes 2097152 | tf_op jit(solution)/shard_map/all_to_all | solution.py:426
  66.6 24.7 %all-to-all-start.2 = ((bf16[128,32,128]{2,1,0:T(8,128)(2,1)}), bf16[128,32,128]{2,1,0:T(8,128)(2,1)S(1)}, u32[]{:S(2)}, u32[]{:S(2)}) async-start(bf16[128,32,128]{2,1,0:T(8,128)(2,1)} %bitcast.40), calls=%async_computation.2 | async-start | bytes 2097152 | tf_op jit(solution)/shard_map/all_to_all | solution.py:426
  91.3 21.1 %all-to-all-start.3 = ((bf16[32,4,32,128]{3,2,1,0:T(8,128)(2,1)}), bf16[32,4,32,128]{3,2,1,0:T(8,128)(2,1)S(1)}, u32[]{:S(2)}, u32[]{:S(2)}) async-start(bf16[32,4,32,128]{3,2,1,0:T(8,128)(2,1)} %copy-done.4), calls=%async_computation.3 | async-start | bytes 2097152 | tf_op jit(solution)/shard_map/all_to_all | solution.py:426
  97.3 7.1 %copy-start.11 = (bf16[512,512]{1,0:T(8,128)(2,1)S(1)}, bf16[512,512]{1,0:T(8,128)(2,1)}, u32[]{:S(2)}) copy-start(bf16[512,512]{1,0:T(8,128)(2,1)} %mix_ref.3) | copy-start | bytes 1572868
  99.0 8.9 %collective-permute-start.12 = (bf16[512,128]{1,0:T(8,128)(2,1)S(1)}, bf16[512,128]{1,0:T(8,128)(2,1)S(1)}, u32[]{:S(2)}, u32[]{:S(2)}) collective-permute-start(bf16[512,128]{1,0:T(8,128)(2,1)S(1)} %get-tuple-element.40), channel_id=1, source_target_pairs={{0,1},{1,2},{2,3},{3,0},{4,5},{5,6},{6,7},{7,4},{8,9},{9,10},{10,1... | collective-permute-start | bytes 393224 | tf_op jit(solution)/shard_map/ppermute | solution.py:437
  100.1 10.3 %collective-permute-start.13 = (bf16[512,128]{1,0:T(8,128)(2,1)S(1)}, bf16[512,128]{1,0:T(8,128)(2,1)S(1)}, u32[]{:S(2)}, u32[]{:S(2)}) collective-permute-start(bf16[512,128]{1,0:T(8,128)(2,1)S(1)} %get-tuple-element.41), channel_id=1, source_target_pairs={{0,2},{1,3},{2,0},{3,1},{4,6},{5,7},{6,4},{7,5},{8,10},{9,11},{10,... | collective-permute-start | bytes 393224 | tf_op jit(solution)/shard_map/ppermute | solution.py:437
  103.3 7.1 %collective-permute-start.14 = (bf16[512,128]{1,0:T(8,128)(2,1)S(1)}, bf16[512,128]{1,0:T(8,128)(2,1)S(1)}, u32[]{:S(2)}, u32[]{:S(2)}) collective-permute-start(bf16[512,128]{1,0:T(8,128)(2,1)S(1)} %get-tuple-element.42), channel_id=1, source_target_pairs={{0,3},{1,0},{2,1},{3,2},{4,7},{5,4},{6,5},{7,6},{8,11},{9,8},{10,9... | collective-permute-start | bytes 393224 | tf_op jit(solution)/shard_map/ppermute | solution.py:437
  106.4 17.0 %copy-start.1 = (bf16[4096,128]{1,0:T(8,128)(2,1)S(1)}, bf16[4096,128]{1,0:T(8,128)(2,1)}, u32[]{:S(2)}) copy-start(bf16[4096,128]{1,0:T(8,128)(2,1)} %x_ref.1) | copy-start | bytes 3145732
  106.4 16.1 %collective-permute-start.6 = (bf16[1024,128]{1,0:T(8,128)(2,1)}, bf16[1024,128]{1,0:T(8,128)(2,1)}, u32[]{:S(2)}, u32[]{:S(2)}) collective-permute-start(bf16[1024,128]{1,0:T(8,128)(2,1)} %get-tuple-element.34), channel_id=1, source_target_pairs={{0,1},{1,2},{2,3},{3,0},{4,5},{5,6},{6,7},{7,4},{8,9},{9,10},{10,1... | collective-permute-start | bytes 786440 | tf_op jit(solution)/shard_map/ppermute | solution.py:437
  107.3 16.1 %collective-permute-start.7 = (bf16[1024,128]{1,0:T(8,128)(2,1)}, bf16[1024,128]{1,0:T(8,128)(2,1)}, u32[]{:S(2)}, u32[]{:S(2)}) collective-permute-start(bf16[1024,128]{1,0:T(8,128)(2,1)} %get-tuple-element.35), channel_id=1, source_target_pairs={{0,2},{1,3},{2,0},{3,1},{4,6},{5,7},{6,4},{7,5},{8,10},{9,11},{10,... | collective-permute-start | bytes 786440 | tf_op jit(solution)/shard_map/ppermute | solution.py:437
  107.9 15.5 %collective-permute-start.8 = (bf16[1024,128]{1,0:T(8,128)(2,1)}, bf16[1024,128]{1,0:T(8,128)(2,1)}, u32[]{:S(2)}, u32[]{:S(2)}) collective-permute-start(bf16[1024,128]{1,0:T(8,128)(2,1)} %get-tuple-element.36), channel_id=1, source_target_pairs={{0,3},{1,0},{2,1},{3,2},{4,7},{5,4},{6,5},{7,6},{8,11},{9,8},{10,9... | collective-permute-start | bytes 786440 | tf_op jit(solution)/shard_map/ppermute | solution.py:437
  113.4 16.7 %all-to-all-start.4 = ((f32[32,16,128]{2,1,0:T(8,128)}), f32[32,16,128]{2,1,0:T(8,128)}, u32[]{:S(2)}, u32[]{:S(2)}) async-start(f32[32,16,128]{2,1,0:T(8,128)} %bitcast.45), calls=%async_computation.4 | async-start | bytes 524288 | tf_op jit(solution)/shard_map/all_to_all | solution.py:426
  119.7 7.9 %copy-start.3 = (bf16[4096,128]{1,0:T(8,128)(2,1)S(1)}, bf16[4096,128]{1,0:T(8,128)(2,1)}, u32[]{:S(2)}) copy-start(bf16[4096,128]{1,0:T(8,128)(2,1)} %cot_ref.1) | copy-start | bytes 3145732
  119.7 6.0 %collective-permute-start.11 = (f32[32,128]{1,0:T(8,128)S(1)}, f32[32,128]{1,0:T(8,128)S(1)}, u32[]{:S(2)}, u32[]{:S(2)}) collective-permute-start(f32[32,128]{1,0:T(8,128)S(1)} %inner.1), channel_id=1, source_target_pairs={{0,3},{1,0},{2,1},{3,2},{4,7},{5,4},{6,5},{7,6},{8,11},{9,8},{10,9... | collective-permute-start | bytes 49160 | tf_op jit(solution)/shard_map/ppermute | solution.py:437
  121.8 5.2 %collective-permute-start.10 = (f32[32,128]{1,0:T(8,128)S(1)}, f32[32,128]{1,0:T(8,128)S(1)}, u32[]{:S(2)}, u32[]{:S(2)}) collective-permute-start(f32[32,128]{1,0:T(8,128)S(1)} %inner.1), channel_id=1, source_target_pairs={{0,2},{1,3},{2,0},{3,1},{4,6},{5,7},{6,4},{7,5},{8,10},{9,11},{10,... | collective-permute-start | bytes 49160 | tf_op jit(solution)/shard_map/ppermute | solution.py:437
  122.6 5.0 %collective-permute-start.9 = (f32[32,128]{1,0:T(8,128)S(1)}, f32[32,128]{1,0:T(8,128)S(1)}, u32[]{:S(2)}, u32[]{:S(2)}) collective-permute-start(f32[32,128]{1,0:T(8,128)S(1)} %inner.1), channel_id=1, source_target_pairs={{0,1},{1,2},{2,3},{3,0},{4,5},{5,6},{6,7},{7,4},{8,9},{9,10},{10,1... | collective-permute-start | bytes 49160 | tf_op jit(solution)/shard_map/ppermute | solution.py:437
  (9 other events, 15.0 us)

commit v2 on v1

--- a/solution.py
+++ b/solution.py
@@ -373,13 +373,29 @@
     )(me, hid, mixing)
 
 
+def total_kernel(in_ref, out_ref):
+    out_ref[...] = jnp.sum(in_ref[...], axis=0)
+
+
+def total(a):
+    return pl.pallas_call(
+        total_kernel,
+        out_shape=jax.ShapeDtypeStruct(a.shape[1:], F32),
+        in_specs=[vspec()],
+        out_specs=vspec(),
+        compiler_params=params(),
+        cost_estimate=cost(),
+        name="total",
+    )(a)
+
+
 def inner_kernel(v_ref, xt_ref, gain_ref, out_ref):
-    def one(g, acc):
+    sums = [jnp.zeros((LOCAL, LANES), F32) for _ in range(NCH)]
+    for g in range(SEQ):
         for i in range(NCH):
-            acc = acc + gain_ref[i * SEQ + g] * (v_ref[g, i].astype(F32) * xt_ref[g, i].astype(F32))
-        return acc
-
-    out_ref[...] = lax.fori_loop(0, SEQ, one, jnp.zeros((LOCAL, LANES), F32))
+            both = v_ref[g, i].astype(F32) * xt_ref[g, i].astype(F32)
+            sums[i] = sums[i] + gain_ref[i * SEQ + g] * both
+    out_ref[...] = (sums[0] + sums[1]) + (sums[2] + sums[3])
 
 
 def inner(v, xt, gain):
@@ -509,7 +525,7 @@
     others = [turned(own, k) for k in range(1, ZN)]
     mean = (own + others[0] + others[1] + others[2]) / full
     grad_in = grad_in_of(v, xt, cotangent, inv, mean, norm_gain)
-    weight_grad = jnp.sum(after(wg, grad_in), axis=0).T
+    weight_grad = total(after(wg, grad_in)).T
     layer_out = whole_of(tokens, parts, place)
     return (layer_out, grad_in, weight_grad)
 

time: 133 us -> 132 us (level)
  waiting for transfers between devices: 22.3 us -> 20.2 us
  local copies, waits for them, and re-layouts: 8.12 us -> 9.77 us
  other arithmetic: 9.39 us -> 7.8 us
    ppermute x15, waiting for transfers between devices: 14.2 us -> 12.3 us  [turned(): lax.ppermute(a, 'ch', [(j, (j + by) % ZN) for j in range(ZN)])]
    unnamed x42 -> x46, local copies, waits for them, and re-layouts: 6.84 us -> 8.48 us
    reduce_sum x1 -> x0, other arithmetic: 1.58 us -> none  [per_device(): weight_grad = jnp.sum(after(wg, grad_in), axis=0).T]
  transfers between devices with their start and end apart: 20 -> 20, of which waited for: 10 -> 8; matrix products, arithmetic and copies ran while one was open for 4% -> 5% of each run, Pallas kernels for 27% -> 27%
where the time goes in v2:
time: 132 us; the launch traced here: 131 us
  starting transfers between devices  56.1 us (42%)
  Pallas kernels  35.9 us (27%)
  waiting for transfers between devices  20.2 us (15%)
  local copies, waits for them, and re-layouts  9.77 us (7%)
  other arithmetic  7.8 us (6%)
    all_to_all x5, starting transfers between devices, exchange(): return lax.all_to_all(a, axes, 0, 0, tiled=True)  33.5 us
    ppermute x15, starting transfers between devices, turned(): lax.ppermute(a, 'ch', [(j, (j + by) % ZN) for j in range(ZN)])  22.5 us
    ppermute x15, waiting for transfers between devices, turned(): lax.ppermute(a, 'ch', [(j, (j + by) % ZN) for j in range(ZN)])  12.3 us
    pallas_call x1, Pallas kernels, forward(): pl.pallas_call(functools.partial(forward_kernel, FWD), out_shape=(jax.Sha...  11.1 us
    pallas_call x1, Pallas kernels, backward(): pl.pallas_call(functools.partial(backward_kernel, BWD), out_shape=jax.Sha...  10.9 us
    unnamed x46, local copies, waits for them, and re-layouts  8.48 us
    all_to_all x5, waiting for transfers between devices, exchange(): return lax.all_to_all(a, axes, 0, 0, tiled=True)  7.87 us
  transfers between devices with their start and end apart: 20, of which 8 were waited for; matrix products, arithmetic and copies ran while one was open for 5% of the time, Pallas kernels for 27%

profile of v2, /device:TPU:2, one launch (start us, length us, event | category | flops | bytes accessed | tf_op | source)
XLA Modules:
  0.0 130.8 jit_solution(10852154186157162417)
XLA Ops:
  0.6 1.8 %multiply_reduce_fusion = f32[4096]{0:T(1024)S(1)} fusion(bf16[4096,128]{1,0:T(8,128)(2,1)} %x_ref.1), kind=kLoop, calls=%fused_computation.1 | loop fusion | flops 1568768 | bytes 1064960 | tf_op jit(solution)/shard_map/reduce_sum | solution.py:502
  2.5 4.1 %collective-permute-start.2 = (f32[32,128]{1,0:T(8,128)S(1)}, f32[32,128]{1,0:T(8,128)S(1)}, u32[]{:S(2)}, u32[]{:S(2)}) collective-permute-start(f32[32,128]{1,0:T(8,128)S(1)} %bitcast.49), channel_id=1, source_target_pairs={{0,3},{1,0},{2,1},{3,2},{4,7},{5,4},{6,5},{7,6},{8,11},{9,8},{10,9... | collective-permute-start | bytes 49160 | tf_op jit(solution)/shard_map/ppermute | solution.py:453
  6.6 1.3 collective-permute-start
  9.7 2.1 %collective-permute-done.1 = f32[32,128]{1,0:T(8,128)S(1)} collective-permute-done((f32[32,128]{1,0:T(8,128)S(1)}, f32[32,128]{1,0:T(8,128)S(1)}, u32[]{:S(2)}, u32[]{:S(2)}) %collective-permute-start.1) | collective-permute-done | bytes 16416 | tf_op jit(solution)/shard_map/ppermute | solution.py:453
  11.9 1.3 %multiply_convert_fusion = f16[32,4,32,128]{3,2,1,0:T(8,128)(2,1)} fusion(bf16[32,4,32,128]{3,2,1,0:T(8,128)(2,1)S(1)} %turn.1.xt_ref, f32[32,128]{1,0:T(8,128)S(1)} %get-tuple-element.45), kind=kLoop, calls=%fused_computation | loop fusion | flops 1572864 | bytes 2113536 | tf_op jit(solution)/shard_map/convert_element_type | solution.py:506
  13.2 7.8 %all-to-all-start = ((f16[32,4,32,128]{3,2,1,0:T(8,128)(2,1)}), f16[32,4,32,128]{3,2,1,0:T(8,128)(2,1)}, u32[]{:S(2)}, u32[]{:S(2)}) async-start(f16[32,4,32,128]{3,2,1,0:T(8,128)(2,1)} %multiply_convert_fusion), calls=%async_computation | async-start | bytes 2097152 | tf_op jit(solution)/shard_map/all_to_all | solution.py:442
  22.0 2.0 %collective-permute-start.4 = (bf16[1024,128]{1,0:T(8,128)(2,1)}, bf16[1024,128]{1,0:T(8,128)(2,1)S(1)}, u32[]{:S(2)}, u32[]{:S(2)}) collective-permute-start(bf16[1024,128]{1,0:T(8,128)(2,1)} %bitcast.9), channel_id=1, source_target_pairs={{0,2},{1,3},{2,0},{3,1},{4,6},{5,7},{6,4},{7,5},{8,10},{9,11},{10,... | collective-permute-start | bytes 786440 | tf_op jit(solution)/shard_map/ppermute | solution.py:453
  26.1 1.3 %prepare.1 = (s32[32,4,8,128]{3,2,1,0:T(8,128)S(1)}, f32[32,128]{1,0:T(8,128)S(1)}) custom-call(s32[16]{0:T(128)S(1)} %copy-done.22, f32[15,2,128]{2,1,0:T(2,128)S(1)} %copy-done.18, f32[15,2,128]{2,1,0:T(2,128)S(1)} %copy-done.19, f32[16,128]{1,0:T(8,128)S(1)} %copy-done.20, f32[1,128]{1,0:T(1,128)S(1)} %bitcast.44), custom_call_target="tpu_custom_call" | custom-call | flops 1000 | bytes 1000 | tf_op jit(solution)/shard_map/prepare/pallas_call | solution.py:106
  27.8 5.1 %collective-permute-done.4.refs_2_ = bf16[1024,128]{1,0:T(8,128)(2,1)S(1)} collective-permute-done((bf16[1024,128]{1,0:T(8,128)(2,1)}, bf16[1024,128]{1,0:T(8,128)(2,1)S(1)}, u32[]{:S(2)}, u32[]{:S(2)}) %collective-permute-start.4) | collective-permute-done | bytes 262176 | tf_op jit(solution)/shard_map/ppermute | solution.py:453
  32.9 2.9 %collective-permute-done.5.refs_3_ = bf16[1024,128]{1,0:T(8,128)(2,1)S(1)} collective-permute-done((bf16[1024,128]{1,0:T(8,128)(2,1)}, bf16[1024,128]{1,0:T(8,128)(2,1)S(1)}, u32[]{:S(2)}, u32[]{:S(2)}) %collective-permute-start.5) | collective-permute-done | bytes 262176 | tf_op jit(solution)/shard_map/ppermute | solution.py:453
  35.8 1.9 %collective-permute-done.3.refs_1_ = bf16[1024,128]{1,0:T(8,128)(2,1)S(1)} collective-permute-done((bf16[1024,128]{1,0:T(8,128)(2,1)}, bf16[1024,128]{1,0:T(8,128)(2,1)S(1)}, u32[]{:S(2)}, u32[]{:S(2)}) %collective-permute-start.3) | collective-permute-done | bytes 262176 | tf_op jit(solution)/shard_map/ppermute | solution.py:453
  37.7 2.0 %grad_hidden.1 = bf16[128,32,128]{2,1,0:T(8,128)(2,1)} custom-call(s32[1]{0:T(128)} %bitcast.me_ref, bf16[512,512]{1,0:T(8,128)(2,1)S(1)} %copy-done.10, bf16[1024,128]{1,0:T(8,128)(2,1)S(1)} %bitcast.38, bf16[1024,128]{1,0:T(8,128)(2,1)S(1)} %collective-permute-done.3.refs_1_, bf16[1024,128]{1,0:T(8,128)(2,1)S(1)} %collective-permute-done.4.refs_2_, ...), custom_call_target="tpu_custom_call" | custom-call | flops 1000 | bytes 1000 | tf_op jit(solution)/shard_map/grad_hidden/pallas_call | solution.py:144
  39.7 8.3 %all-to-all-start.1 = ((bf16[128,32,128]{2,1,0:T(8,128)(2,1)}), bf16[128,32,128]{2,1,0:T(8,128)(2,1)S(1)}, u32[]{:S(2)}, u32[]{:S(2)}) async-start(bf16[128,32,128]{2,1,0:T(8,128)(2,1)} %grad_hidden.1), calls=%async_computation.1 | async-start | bytes 2097152 | tf_op jit(solution)/shard_map/all_to_all | solution.py:442
  48.0 1.5 %convert_element_type.24.x_ref = f32[32,4,32,128]{3,2,1,0:T(8,128)S(1)} convert(f16[32,4,32,128]{3,2,1,0:T(8,128)(2,1)} %all-to-all-done) | non-fusion elementwise | flops 524288 | bytes 3145728 | tf_op jit(solution)/shard_map/convert_element_type | solution.py:508
  49.5 11.1 %forward.1 = (bf16[32,4,32,128]{3,2,1,0:T(8,128)(2,1)S(1)}, f32[4,32,4,8,128]{4,3,2,1,0:T(8,128)S(1)}) custom-call(f32[32,4,32,128]{3,2,1,0:T(8,128)S(1)} %convert_element_type.24.x_ref, s32[32,4,8,128]{3,2,1,0:T(8,128)S(1)} %get-tuple-element.24.rel_ref, f32[128]{0:T(128)S(1)} %reshape.67.t_ref), custom_call_target="tpu_custom_call" | custom-call | flops 1000 | bytes 1000 | tf_op jit(solution)/shard_map/forward/pallas_call | solution.py:216
  60.6 1.3 %copy-done.6 = f32[4,32,4,8,128]{4,3,2,1,0:T(8,128)} copy-done((f32[4,32,4,8,128]{4,3,2,1,0:T(8,128)}, f32[4,32,4,8,128]{4,3,2,1,0:T(8,128)S(1)}, u32[]{:S(2)}) %copy-start.6) | copy-done | bytes 2097176
  62.9 3.6 %all-to-all-done.1 = bf16[128,32,128]{2,1,0:T(8,128)(2,1)S(1)} async-done(((bf16[128,32,128]{2,1,0:T(8,128)(2,1)}), bf16[128,32,128]{2,1,0:T(8,128)(2,1)S(1)}, u32[]{:S(2)}, u32[]{:S(2)}) %all-to-all-start.1) | async-done | bytes 1048608 | tf_op jit(solution)/shard_map/all_to_all | solution.py:442
  66.6 6.1 %all-to-all-start.2 = ((bf16[128,32,128]{2,1,0:T(8,128)(2,1)}), bf16[128,32,128]{2,1,0:T(8,128)(2,1)S(1)}, u32[]{:S(2)}, u32[]{:S(2)}) async-start(bf16[128,32,128]{2,1,0:T(8,128)(2,1)} %bitcast.40), calls=%async_computation.2 | async-start | bytes 2097152 | tf_op jit(solution)/shard_map/all_to_all | solution.py:442
  72.7 2.4 %pad_maximum_fusion.held_ref = bf16[4,1024,128]{2,1,0:T(8,128)(2,1)} fusion(bf16[1,1024,128]{2,1,0:T(8,128)(2,1)} %bitcast.42, bf16[1,1024,128]{2,1,0:T(8,128)(2,1)} %bitcast.41, bf16[1,1024,128]{2,1,0:T(8,128)(2,1)} %bitcast.43, bf16[1,1024,128]{2,1,0:T(8,128)(2,1)S(1)} %bitcast.39), kind=kLoop, calls=%fused_computation.2 | loop fusion | flops 1572864 | bytes 2097152 | tf_op jit(solution)/shard_map/stack | solution.py:513
  76.1 10.9 %backward.1 = bf16[32,4,32,128]{3,2,1,0:T(8,128)(2,1)S(1)} custom-call(bf16[32,4,32,128]{3,2,1,0:T(8,128)(2,1)S(1)} %bitcast.37, f32[4,32,4,8,128]{4,3,2,1,0:T(8,128)S(1)} %copy-done.7, s32[32,4,8,128]{3,2,1,0:T(8,128)S(1)} %copy-done.9, f32[128]{0:T(128)S(1)} %reshape.67.t_ref), custom_call_target="tpu_custom_call" | custom-call | flops 1000 | bytes 1000 | tf_op jit(solution)/shard_map/backward/pallas_call | solution.py:288
  88.0 3.3 %all-to-all-done.2.hid_ref = bf16[128,32,128]{2,1,0:T(8,128)(2,1)S(1)} async-done(((bf16[128,32,128]{2,1,0:T(8,128)(2,1)}), bf16[128,32,128]{2,1,0:T(8,128)(2,1)S(1)}, u32[]{:S(2)}, u32[]{:S(2)}) %all-to-all-start.2) | async-done | bytes 1048608 | tf_op jit(solution)/shard_map/all_to_all | solution.py:442
  91.3 4.8 %all-to-all-start.3 = ((bf16[32,4,32,128]{3,2,1,0:T(8,128)(2,1)}), bf16[32,4,32,128]{3,2,1,0:T(8,128)(2,1)S(1)}, u32[]{:S(2)}, u32[]{:S(2)}) async-start(bf16[32,4,32,128]{3,2,1,0:T(8,128)(2,1)} %copy-done.4), calls=%async_computation.3 | async-start | bytes 2097152 | tf_op jit(solution)/shard_map/all_to_all | solution.py:442
  97.3 1.6 %weigh.1 = (f32[512,128]{1,0:T(8,128)S(1)}, bf16[512,128]{1,0:T(8,128)(2,1)S(1)}, bf16[512,128]{1,0:T(8,128)(2,1)S(1)}, bf16[512,128]{1,0:T(8,128)(2,1)S(1)}) custom-call(s32[1]{0:T(128)} %bitcast.me_ref, bf16[128,32,128]{2,1,0:T(8,128)(2,1)S(1)} %all-to-all-done.2.hid_ref, bf16[4,1024,128]{2,1,0:T(8,128)(2,1)S(1)} %copy-done.5), custom_call_target="tpu_custom_call" | custom-call | flops 1000 | bytes 1000 | tf_op jit(solution)/shard_map/weigh/pallas_call | solution.py:336
  100.0 3.2 %collective-permute-start.13 = (bf16[512,128]{1,0:T(8,128)(2,1)S(1)}, bf16[512,128]{1,0:T(8,128)(2,1)S(1)}, u32[]{:S(2)}, u32[]{:S(2)}) collective-permute-start(bf16[512,128]{1,0:T(8,128)(2,1)S(1)} %get-tuple-element.41), channel_id=1, source_target_pairs={{0,2},{1,3},{2,0},{3,1},{4,6},{5,7},{6,4},{7,5},{8,10},{9,11},{10,... | collective-permute-start | bytes 393224 | tf_op jit(solution)/shard_map/ppermute | solution.py:453
  104.4 2.0 %mix.1 = (bf16[1024,128]{1,0:T(8,128)(2,1)S(1)}, bf16[1024,128]{1,0:T(8,128)(2,1)}, bf16[1024,128]{1,0:T(8,128)(2,1)}, bf16[1024,128]{1,0:T(8,128)(2,1)}) custom-call(s32[1]{0:T(128)} %bitcast.me_ref, bf16[128,32,128]{2,1,0:T(8,128)(2,1)S(1)} %all-to-all-done.2.hid_ref, bf16[512,512]{1,0:T(8,128)(2,1)S(1)} %copy-done.11), custom_call_target="tpu_custom_call" | custom-call | flops 1000 | bytes 1000 | tf_op jit(solution)/shard_map/mix/pallas_call | solution.py:364
  108.6 2.0 %collective-permute-start.8 = (bf16[1024,128]{1,0:T(8,128)(2,1)}, bf16[1024,128]{1,0:T(8,128)(2,1)}, u32[]{:S(2)}, u32[]{:S(2)}) collective-permute-start(bf16[1024,128]{1,0:T(8,128)(2,1)} %get-tuple-element.36), channel_id=1, source_target_pairs={{0,3},{1,0},{2,1},{3,2},{4,7},{5,4},{6,5},{7,6},{8,11},{9,8},{10,9... | collective-permute-start | bytes 786440 | tf_op jit(solution)/shard_map/ppermute | solution.py:453
  113.2 6.5 %all-to-all-start.4 = ((f32[32,16,128]{2,1,0:T(8,128)}), f32[32,16,128]{2,1,0:T(8,128)S(1)}, u32[]{:S(2)}, u32[]{:S(2)}) async-start(f32[32,16,128]{2,1,0:T(8,128)} %bitcast.45), calls=%async_computation.4 | async-start | bytes 524288 | tf_op jit(solution)/shard_map/all_to_all | solution.py:442
  119.7 1.5 %collective-permute-start.11 = (f32[32,128]{1,0:T(8,128)S(1)}, f32[32,128]{1,0:T(8,128)S(1)}, u32[]{:S(2)}, u32[]{:S(2)}) collective-permute-start(f32[32,128]{1,0:T(8,128)S(1)} %inner.1), channel_id=1, source_target_pairs={{0,3},{1,0},{2,1},{3,2},{4,7},{5,4},{6,5},{7,6},{8,11},{9,8},{10,9... | collective-permute-start | bytes 49160 | tf_op jit(solution)/shard_map/ppermute | solution.py:453
  121.2 1.3 %collective-permute-start.10 = (f32[32,128]{1,0:T(8,128)S(1)}, f32[32,128]{1,0:T(8,128)S(1)}, u32[]{:S(2)}, u32[]{:S(2)}) collective-permute-start(f32[32,128]{1,0:T(8,128)S(1)} %inner.1), channel_id=1, source_target_pairs={{0,2},{1,3},{2,0},{3,1},{4,6},{5,7},{6,4},{7,5},{8,10},{9,11},{10,... | collective-permute-start | bytes 49160 | tf_op jit(solution)/shard_map/ppermute | solution.py:453
  122.6 1.3 %collective-permute-start.9 = (f32[32,128]{1,0:T(8,128)S(1)}, f32[32,128]{1,0:T(8,128)S(1)}, u32[]{:S(2)}, u32[]{:S(2)}) collective-permute-start(f32[32,128]{1,0:T(8,128)S(1)} %inner.1), channel_id=1, source_target_pairs={{0,1},{1,2},{2,3},{3,0},{4,5},{5,6},{6,7},{7,4},{8,9},{9,10},{10,1... | collective-permute-start | bytes 49160 | tf_op jit(solution)/shard_map/ppermute | solution.py:453
  124.9 2.3 %whole.1 = bf16[8,4,128,128]{3,2,1,0:T(8,128)(2,1)} custom-call(s32[1]{0:T(128)} %bitcast.me_ref, bf16[8,4,128,128]{3,2,1,0:T(8,128)(2,1)S(1)} %bitcast.35, bf16[1024,128]{1,0:T(8,128)(2,1)S(1)} %copy-done.17, bf16[1024,128]{1,0:T(8,128)(2,1)} %collective-permute-done.6.refs_1_, bf16[1024,128]{1,0:T(8,128)(2,1)} %collective-permute-done.7.refs_2_, ...), custom_call_target="tpu_custom_call" | custom-call | flops 1000 | bytes 1000 | tf_op jit(solution)/shard_map/whole/pallas_call | solution.py:477
  127.5 2.6 %grad_in.1 = bf16[4096,128]{1,0:T(8,128)(2,1)} custom-call(bf16[32,4,32,128]{3,2,1,0:T(8,128)(2,1)S(1)} %all-to-all-done.3.v_ref, bf16[32,4,32,128]{3,2,1,0:T(8,128)(2,1)S(1)} %turn.1.xt_ref, bf16[4096,128]{1,0:T(8,128)(2,1)S(1)} %copy-done.3, f32[32,128]{1,0:T(8,128)S(1)} %get-tuple-element.46.inv_ref, f32[32,128]{1,0:T(8,128)S(1)} %add_multiply_fusion.1.mean_ref, ...), custom_call_target="tpu_custom_call" | custom-call | flops 1000 | bytes 1000 | tf_op jit(solution)/shard_map/grad_in/pallas_call | solution.py:429
  (77 shorter events, 18.5 us)
Async XLA Ops:
  2.5 7.3 %collective-permute-start.2 = (f32[32,128]{1,0:T(8,128)S(1)}, f32[32,128]{1,0:T(8,128)S(1)}, u32[]{:S(2)}, u32[]{:S(2)}) collective-permute-start(f32[32,128]{1,0:T(8,128)S(1)} %bitcast.49), channel_id=1, source_target_pairs={{0,3},{1,0},{2,1},{3,2},{4,7},{5,4},{6,5},{7,6},{8,11},{9,8},{10,9... | collective-permute-start | bytes 49160 | tf_op jit(solution)/shard_map/ppermute | solution.py:453
  6.6 5.2 %collective-permute-start.1 = (f32[32,128]{1,0:T(8,128)S(1)}, f32[32,128]{1,0:T(8,128)S(1)}, u32[]{:S(2)}, u32[]{:S(2)}) collective-permute-start(f32[32,128]{1,0:T(8,128)S(1)} %bitcast.50), channel_id=1, source_target_pairs={{0,2},{1,3},{2,0},{3,1},{4,6},{5,7},{6,4},{7,5},{8,10},{9,11},{10,... | collective-permute-start | bytes 49160 | tf_op jit(solution)/shard_map/ppermute | solution.py:453
  6.6 5.2 %collective-permute-start = (f32[32,128]{1,0:T(8,128)S(1)}, f32[32,128]{1,0:T(8,128)S(1)}, u32[]{:S(2)}, u32[]{:S(2)}) collective-permute-start(f32[32,128]{1,0:T(8,128)S(1)} %bitcast.51), channel_id=1, source_target_pairs={{0,1},{1,2},{2,3},{3,0},{4,5},{5,6},{6,7},{7,4},{8,9},{9,10},{10,1... | collective-permute-start | bytes 49160 | tf_op jit(solution)/shard_map/ppermute | solution.py:453
  11.9 9.2 %copy-start.2 = (bf16[4096,128]{1,0:T(8,128)(2,1)S(1)}, bf16[4096,128]{1,0:T(8,128)(2,1)}, u32[]{:S(2)}) copy-start(bf16[4096,128]{1,0:T(8,128)(2,1)} %cot_ref.1) | copy-start | bytes 3145732
  13.2 12.9 %copy-start.18 = (f32[15,2,128]{2,1,0:T(2,128)S(1)}, f32[15,2,128]{2,1,0:T(2,128)}, u32[]{:S(2)}) copy-start(f32[15,2,128]{2,1,0:T(2,128)} %low_ref.1) | copy-start | bytes 46084
  13.2 12.9 %copy-start.19 = (f32[15,2,128]{2,1,0:T(2,128)S(1)}, f32[15,2,128]{2,1,0:T(2,128)}, u32[]{:S(2)}) copy-start(f32[15,2,128]{2,1,0:T(2,128)} %high_ref.1) | copy-start | bytes 46084
  13.2 12.9 %copy-start.20 = (f32[16,128]{1,0:T(8,128)S(1)}, f32[16,128]{1,0:T(8,128)}, u32[]{:S(2)}) copy-start(f32[16,128]{1,0:T(8,128)} %level_ref.1) | copy-start | bytes 24580
  13.2 12.9 %copy-start.21 = (f32[128]{0:T(128)S(1)}, f32[128]{0:T(128)}, u32[]{:S(2)}) copy-start(f32[128]{0:T(128)} %gain_ref.3) | copy-start | bytes 1540
  13.2 12.9 %copy-start.22 = (s32[16]{0:T(128)S(1)}, s32[16]{0:T(128)}, u32[]{:S(2)}) copy-start(s32[16]{0:T(128)} %len_ref.1) | copy-start | bytes 196
  13.2 24.5 %copy-start.10 = (bf16[512,512]{1,0:T(8,128)(2,1)S(1)}, bf16[512,512]{1,0:T(8,128)(2,1)}, u32[]{:S(2)}) copy-start(bf16[512,512]{1,0:T(8,128)(2,1)} %mix_ref.3) | copy-start | bytes 1572868
  13.2 26.5 %all-to-all-start = ((f16[32,4,32,128]{3,2,1,0:T(8,128)(2,1)}), f16[32,4,32,128]{3,2,1,0:T(8,128)(2,1)}, u32[]{:S(2)}, u32[]{:S(2)}) async-start(f16[32,4,32,128]{3,2,1,0:T(8,128)(2,1)} %multiply_convert_fusion), calls=%async_computation | async-start | bytes 2097152 | tf_op jit(solution)/shard_map/all_to_all | solution.py:442
  22.0 10.9 %collective-permute-start.4 = (bf16[1024,128]{1,0:T(8,128)(2,1)}, bf16[1024,128]{1,0:T(8,128)(2,1)S(1)}, u32[]{:S(2)}, u32[]{:S(2)}) collective-permute-start(bf16[1024,128]{1,0:T(8,128)(2,1)} %bitcast.9), channel_id=1, source_target_pairs={{0,2},{1,3},{2,0},{3,1},{4,6},{5,7},{6,4},{7,5},{8,10},{9,11},{10,... | collective-permute-start | bytes 786440 | tf_op jit(solution)/shard_map/ppermute | solution.py:453
  24.0 11.8 %collective-permute-start.5 = (bf16[1024,128]{1,0:T(8,128)(2,1)}, bf16[1024,128]{1,0:T(8,128)(2,1)S(1)}, u32[]{:S(2)}, u32[]{:S(2)}) collective-permute-start(bf16[1024,128]{1,0:T(8,128)(2,1)} %bitcast.10), channel_id=1, source_target_pairs={{0,3},{1,0},{2,1},{3,2},{4,7},{5,4},{6,5},{7,6},{8,11},{9,8},{10,9... | collective-permute-start | bytes 786440 | tf_op jit(solution)/shard_map/ppermute | solution.py:453
  24.9 12.9 %collective-permute-start.3 = (bf16[1024,128]{1,0:T(8,128)(2,1)}, bf16[1024,128]{1,0:T(8,128)(2,1)S(1)}, u32[]{:S(2)}, u32[]{:S(2)}) collective-permute-start(bf16[1024,128]{1,0:T(8,128)(2,1)} %bitcast.8), channel_id=1, source_target_pairs={{0,1},{1,2},{2,3},{3,0},{4,5},{5,6},{6,7},{7,4},{8,9},{9,10},{10,1... | collective-permute-start | bytes 786440 | tf_op jit(solution)/shard_map/ppermute | solution.py:453
  27.4 22.1 %copy-start.8 = (s32[32,4,8,128]{3,2,1,0:T(8,128)}, s32[32,4,8,128]{3,2,1,0:T(8,128)S(1)}, u32[]{:S(2)}) copy-start(s32[32,4,8,128]{3,2,1,0:T(8,128)S(1)} %get-tuple-element.24.rel_ref) | copy-start | bytes 1572868
  32.9 6.8 %copy-start.13 = (bf16[1024,128]{1,0:T(8,128)(2,1)}, bf16[1024,128]{1,0:T(8,128)(2,1)S(1)}, u32[]{:S(2)}) copy-start(bf16[1024,128]{1,0:T(8,128)(2,1)S(1)} %collective-permute-done.4.refs_2_) | copy-start | bytes 786436
  39.7 26.9 %all-to-all-start.1 = ((bf16[128,32,128]{2,1,0:T(8,128)(2,1)}), bf16[128,32,128]{2,1,0:T(8,128)(2,1)S(1)}, u32[]{:S(2)}, u32[]{:S(2)}) async-start(bf16[128,32,128]{2,1,0:T(8,128)(2,1)} %grad_hidden.1), calls=%async_computation.1 | async-start | bytes 2097152 | tf_op jit(solution)/shard_map/all_to_all | solution.py:442
  66.6 24.7 %all-to-all-start.2 = ((bf16[128,32,128]{2,1,0:T(8,128)(2,1)}), bf16[128,32,128]{2,1,0:T(8,128)(2,1)S(1)}, u32[]{:S(2)}, u32[]{:S(2)}) async-start(bf16[128,32,128]{2,1,0:T(8,128)(2,1)} %bitcast.40), calls=%async_computation.2 | async-start | bytes 2097152 | tf_op jit(solution)/shard_map/all_to_all | solution.py:442
  91.3 21.1 %all-to-all-start.3 = ((bf16[32,4,32,128]{3,2,1,0:T(8,128)(2,1)}), bf16[32,4,32,128]{3,2,1,0:T(8,128)(2,1)S(1)}, u32[]{:S(2)}, u32[]{:S(2)}) async-start(bf16[32,4,32,128]{3,2,1,0:T(8,128)(2,1)} %copy-done.4), calls=%async_computation.3 | async-start | bytes 2097152 | tf_op jit(solution)/shard_map/all_to_all | solution.py:442
  97.3 7.1 %copy-start.11 = (bf16[512,512]{1,0:T(8,128)(2,1)S(1)}, bf16[512,512]{1,0:T(8,128)(2,1)}, u32[]{:S(2)}) copy-start(bf16[512,512]{1,0:T(8,128)(2,1)} %mix_ref.3) | copy-start | bytes 1572868
  99.0 9.6 %collective-permute-start.12 = (bf16[512,128]{1,0:T(8,128)(2,1)S(1)}, bf16[512,128]{1,0:T(8,128)(2,1)S(1)}, u32[]{:S(2)}, u32[]{:S(2)}) collective-permute-start(bf16[512,128]{1,0:T(8,128)(2,1)S(1)} %get-tuple-element.40), channel_id=1, source_target_pairs={{0,1},{1,2},{2,3},{3,0},{4,5},{5,6},{6,7},{7,4},{8,9},{9,10},{10,1... | collective-permute-start | bytes 393224 | tf_op jit(solution)/shard_map/ppermute | solution.py:453
  100.0 10.6 %collective-permute-start.13 = (bf16[512,128]{1,0:T(8,128)(2,1)S(1)}, bf16[512,128]{1,0:T(8,128)(2,1)S(1)}, u32[]{:S(2)}, u32[]{:S(2)}) collective-permute-start(bf16[512,128]{1,0:T(8,128)(2,1)S(1)} %get-tuple-element.41), channel_id=1, source_target_pairs={{0,2},{1,3},{2,0},{3,1},{4,6},{5,7},{6,4},{7,5},{8,10},{9,11},{10,... | collective-permute-start | bytes 393224 | tf_op jit(solution)/shard_map/ppermute | solution.py:453
  103.2 7.4 %collective-permute-start.14 = (bf16[512,128]{1,0:T(8,128)(2,1)S(1)}, bf16[512,128]{1,0:T(8,128)(2,1)S(1)}, u32[]{:S(2)}, u32[]{:S(2)}) collective-permute-start(bf16[512,128]{1,0:T(8,128)(2,1)S(1)} %get-tuple-element.42), channel_id=1, source_target_pairs={{0,3},{1,0},{2,1},{3,2},{4,7},{5,4},{6,5},{7,6},{8,11},{9,8},{10,9... | collective-permute-start | bytes 393224 | tf_op jit(solution)/shard_map/ppermute | solution.py:453
  107.1 16.8 %copy-start.1 = (bf16[4096,128]{1,0:T(8,128)(2,1)S(1)}, bf16[4096,128]{1,0:T(8,128)(2,1)}, u32[]{:S(2)}) copy-start(bf16[4096,128]{1,0:T(8,128)(2,1)} %x_ref.1) | copy-start | bytes 3145732
  107.1 15.4 %collective-permute-start.6 = (bf16[1024,128]{1,0:T(8,128)(2,1)}, bf16[1024,128]{1,0:T(8,128)(2,1)}, u32[]{:S(2)}, u32[]{:S(2)}) collective-permute-start(bf16[1024,128]{1,0:T(8,128)(2,1)} %get-tuple-element.34), channel_id=1, source_target_pairs={{0,1},{1,2},{2,3},{3,0},{4,5},{5,6},{6,7},{7,4},{8,9},{9,10},{10,1... | collective-permute-start | bytes 786440 | tf_op jit(solution)/shard_map/ppermute | solution.py:453
  107.9 15.9 %collective-permute-start.7 = (bf16[1024,128]{1,0:T(8,128)(2,1)}, bf16[1024,128]{1,0:T(8,128)(2,1)}, u32[]{:S(2)}, u32[]{:S(2)}) collective-permute-start(bf16[1024,128]{1,0:T(8,128)(2,1)} %get-tuple-element.35), channel_id=1, source_target_pairs={{0,2},{1,3},{2,0},{3,1},{4,6},{5,7},{6,4},{7,5},{8,10},{9,11},{10,... | collective-permute-start | bytes 786440 | tf_op jit(solution)/shard_map/ppermute | solution.py:453
  108.6 15.3 %collective-permute-start.8 = (bf16[1024,128]{1,0:T(8,128)(2,1)}, bf16[1024,128]{1,0:T(8,128)(2,1)}, u32[]{:S(2)}, u32[]{:S(2)}) collective-permute-start(bf16[1024,128]{1,0:T(8,128)(2,1)} %get-tuple-element.36), channel_id=1, source_target_pairs={{0,3},{1,0},{2,1},{3,2},{4,7},{5,4},{6,5},{7,6},{8,11},{9,8},{10,9... | collective-permute-start | bytes 786440 | tf_op jit(solution)/shard_map/ppermute | solution.py:453
  113.2 16.9 %all-to-all-start.4 = ((f32[32,16,128]{2,1,0:T(8,128)}), f32[32,16,128]{2,1,0:T(8,128)S(1)}, u32[]{:S(2)}, u32[]{:S(2)}) async-start(f32[32,16,128]{2,1,0:T(8,128)} %bitcast.45), calls=%async_computation.4 | async-start | bytes 524288 | tf_op jit(solution)/shard_map/all_to_all | solution.py:442
  119.7 7.8 %copy-start.3 = (bf16[4096,128]{1,0:T(8,128)(2,1)S(1)}, bf16[4096,128]{1,0:T(8,128)(2,1)}, u32[]{:S(2)}) copy-start(bf16[4096,128]{1,0:T(8,128)(2,1)} %cot_ref.1) | copy-start | bytes 3145732
  119.7 7.4 %collective-permute-start.11 = (f32[32,128]{1,0:T(8,128)S(1)}, f32[32,128]{1,0:T(8,128)S(1)}, u32[]{:S(2)}, u32[]{:S(2)}) collective-permute-start(f32[32,128]{1,0:T(8,128)S(1)} %inner.1), channel_id=1, source_target_pairs={{0,3},{1,0},{2,1},{3,2},{4,7},{5,4},{6,5},{7,6},{8,11},{9,8},{10,9... | collective-permute-start | bytes 49160 | tf_op jit(solution)/shard_map/ppermute | solution.py:453
  121.2 6.0 %collective-permute-start.10 = (f32[32,128]{1,0:T(8,128)S(1)}, f32[32,128]{1,0:T(8,128)S(1)}, u32[]{:S(2)}, u32[]{:S(2)}) collective-permute-start(f32[32,128]{1,0:T(8,128)S(1)} %inner.1), channel_id=1, source_target_pairs={{0,2},{1,3},{2,0},{3,1},{4,6},{5,7},{6,4},{7,5},{8,10},{9,11},{10,... | collective-permute-start | bytes 49160 | tf_op jit(solution)/shard_map/ppermute | solution.py:453
  122.6 5.0 %collective-permute-start.9 = (f32[32,128]{1,0:T(8,128)S(1)}, f32[32,128]{1,0:T(8,128)S(1)}, u32[]{:S(2)}, u32[]{:S(2)}) collective-permute-start(f32[32,128]{1,0:T(8,128)S(1)} %inner.1), channel_id=1, source_target_pairs={{0,1},{1,2},{2,3},{3,0},{4,5},{5,6},{6,7},{7,4},{8,9},{9,10},{10,1... | collective-permute-start | bytes 49160 | tf_op jit(solution)/shard_map/ppermute | solution.py:453
  (11 other events, 16.7 us)
